TPU v7x, 256 devices: a whole 4x4x8 slice. The times are simulated.
256 devices in a mesh: ctx: 16 (over z_lo, y), ep: 16 (over z_hi, x, core).
Axes of the slice: x: 4, y: 4, z: 8 (z_hi: 2, z_lo: 4; z = z_hi * 4 + z_lo), core: 2. Of those that a mesh axis runs over, the one named last changes fastest.
Arguments:
- queries: bfloat16 [4096, 8192], P('ctx', 'ep'), may hold values from -80 to 80
- key_states: bfloat16 [4096, 512], P('ctx'), may hold values from -4 to 4
- value_head_states: bfloat16 [4096, 512], P('ctx'), may hold values from -6 to 6
- block_order: int32 [32], P('ctx'), may hold values from 0 to 31, each once
- out_proj: bfloat16 [8192, 4096], P('ep', 'ctx'), may hold values from -0.0625 to 0.0625
- residual: bfloat16 [4096, 4096], P(('ctx', 'ep')), may hold values from -6 to 6
- norm_gain: float32 [4096], replicated, may hold values from 0.25 to 1.75
- w_gate: bfloat16 [4096, 98304], P(None, ('ctx', 'ep')), may hold values from -0.09375 to 0.09375
- w_up: bfloat16 [4096, 98304], P(None, ('ctx', 'ep')), may hold values from -0.09375 to 0.09375
- w_down: bfloat16 [98304, 4096], P(('ctx', 'ep')), may hold values from -0.21875 to 0.21875
- routes: int32 [4096, 8], P(('ctx', 'ep')), may hold values from 0 to 127, all different within a row; in each aligned block of 16 rows (0 to 15, 16 to 31, ...) at most 3 rows name the same one
- gate_weights: float32 [4096, 8], P(('ctx', 'ep')), may hold values from 0.2 to 0.8
Outputs:
- layer_output: bfloat16 [4096, 4096], P(('ctx', 'ep'))
Inputs may be any that keep to these rules, and one draw needn't show every extreme that they name: `block_order`: each number once. `routes`: 8 different experts a row; in the rows of one device no expert is named by more than 3 rows, a bound that some block reaches.
All inputs are finite; a program needn't handle non-finite values.
Results may differ from a plain program's by a relative error of at most 0.02.
Values may be sent and summed in bfloat16 or wider, within the bound.
A program may use at most 128 MiB of HBM per device.

v0:
```python
import math

import jax
import jax.numpy as jnp
from jax import lax
from jax.sharding import PartitionSpec as P

D = 4096
QUERY_HEADS = 64
KEY_HEADS = 4
HEAD_SIZE = 128
TOP = 8
SPLIT = 2


NEG_FILL = -1e30
EPS = 1e-06


def expert_half(inputs, w_gate, w_up, w_down):
    gate_pre = jnp.dot(inputs, w_gate, preferred_element_type=jnp.float32)
    up_pre = jnp.dot(inputs, w_up, preferred_element_type=jnp.float32)
    hidden_act = (jax.nn.silu(gate_pre) * up_pre).astype(jnp.bfloat16)
    return jnp.dot(hidden_act, w_down, preferred_element_type=jnp.float32).astype(jnp.bfloat16)


def local(
    queries,
    key_states,
    value_head_states,
    block_order,
    out_proj,
    residual,
    norm_gain,
    w_gate,
    w_up,
    w_down,
    routes,
    gate_weights,
):
    span_rows = queries.shape[0]
    half_rows = span_rows // 2
    local_heads = queries.shape[1] // HEAD_SIZE
    ctx_count = lax.axis_size("ctx")
    ep_count = lax.axis_size("ep")
    key_value_index = lax.axis_index("ep") * local_heads // (QUERY_HEADS // KEY_HEADS)
    key_head = lax.dynamic_slice_in_dim(key_states, key_value_index * HEAD_SIZE, HEAD_SIZE, 1)
    value_head = lax.dynamic_slice_in_dim(
        value_head_states, key_value_index * HEAD_SIZE, HEAD_SIZE, 1
    )
    offsets = jnp.arange(half_rows, dtype=jnp.int32)
    own_pos = (block_order[:, None] * half_rows + offsets[None, :]).reshape(-1)
    newest = jnp.max(own_pos)
    grouped = queries.reshape(span_rows, local_heads, HEAD_SIZE)
    score_scale = 1.0 / math.sqrt(HEAD_SIZE)

    def attend_block(carried, block_data):
        key_block, value_block, block_id = block_data

        def update(running):
            run_max, run_sum, run_acc = running
            key_pos = block_id * half_rows + offsets
            allowed = key_pos[None, :] <= own_pos[:, None]
            scores = (
                jnp.einsum("qhd,kd->hqk", grouped, key_block, preferred_element_type=jnp.float32)
                * score_scale
            )
            scores = jnp.where(allowed[None], scores, NEG_FILL)
            new_max = jnp.maximum(run_max, jnp.max(scores, axis=2))
            shrink = jnp.exp(run_max - new_max)
            unnorm = jnp.where(allowed[None], jnp.exp(scores - new_max[:, :, None]), 0.0)
            run_sum = run_sum * shrink + jnp.sum(unnorm, axis=2)
            run_acc = run_acc * shrink[:, :, None] + jnp.einsum(
                "hqk,kd->hqd",
                unnorm.astype(jnp.bfloat16),
                value_block,
                preferred_element_type=jnp.float32,
            )
            return (new_max, run_sum, run_acc)

        def keep_state(running):
            return running

        return (lax.cond(block_id * half_rows <= newest, update, keep_state, carried), None)

    initial = (
        jnp.full((local_heads, span_rows), NEG_FILL, jnp.float32),
        jnp.zeros((local_heads, span_rows), jnp.float32),
        jnp.zeros((local_heads, span_rows, HEAD_SIZE), jnp.float32),
    )
    carried = initial
    key_piece = lax.all_gather(key_head, "ctx", axis=0, tiled=True)
    value_piece = lax.all_gather(value_head, "ctx", axis=0, tiled=True)
    block_piece = lax.all_gather(block_order, "ctx", axis=0, tiled=True)
    blocks_in = block_piece.shape[0]
    stacked_rows = (
        key_piece.reshape(blocks_in, half_rows, HEAD_SIZE),
        value_piece.reshape(blocks_in, half_rows, HEAD_SIZE),
        block_piece,
    )
    carried, ignored = lax.scan(attend_block, carried, stacked_rows)
    run_max, run_sum, run_acc = carried
    attended = (
        (run_acc / run_sum[:, :, None])
        .transpose(1, 0, 2)
        .reshape(span_rows, local_heads * HEAD_SIZE)
        .astype(jnp.bfloat16)
    )
    proj_full = lax.all_gather(out_proj, "ctx", axis=1, tiled=True)
    tok_rows = residual.shape[0]
    group_part = jnp.dot(attended, proj_full, preferred_element_type=jnp.float32).astype(
        jnp.bfloat16
    )
    head_sum = lax.psum_scatter(
        lax.optimization_barrier(group_part).astype(jnp.float32).astype(jnp.bfloat16),
        "ep",
        scatter_dimension=0,
        tiled=True,
    ).astype(jnp.float32)
    hidden_state = (residual.astype(jnp.float32) + head_sum).astype(jnp.bfloat16)
    widened = lax.optimization_barrier(hidden_state).astype(jnp.float32)
    normed = (
        widened * lax.rsqrt(jnp.mean(widened * widened, axis=1, keepdims=True) + EPS) * norm_gain
    ).astype(jnp.bfloat16)
    expert_count = ctx_count * ep_count // SPLIT
    exp_row = ep_count // SPLIT
    capacity = min(tok_rows, max(3, 3 * tok_rows * TOP // (2 * expert_count)))
    route_flat = routes.reshape(-1)
    onehot = (route_flat[:, None] == jnp.arange(expert_count, dtype=jnp.int32)[None, :]).astype(
        jnp.int32
    )
    route_rank = jnp.sum(onehot * (jnp.cumsum(onehot, axis=0) - 1), axis=1)
    sources = jnp.repeat(normed, TOP, axis=0)
    slot_index = route_flat * capacity + route_rank
    packed = jnp.zeros((expert_count * capacity, D), jnp.bfloat16).at[slot_index].set(sources)
    packed = packed.reshape(ctx_count, exp_row, 1, capacity, D)
    packed = jnp.broadcast_to(packed, (ctx_count, exp_row, SPLIT, capacity, D)).reshape(
        ctx_count, ep_count, capacity, D
    )
    arrived = lax.all_to_all(
        lax.all_to_all(packed, "ctx", split_axis=0, concat_axis=0, tiled=True),
        "ep",
        split_axis=1,
        concat_axis=1,
        tiled=True,
    )
    partial_value = expert_half(arrived.reshape(-1, D), w_gate, w_up, w_down).reshape(
        ctx_count, ep_count, capacity, D
    )
    returned = lax.all_to_all(
        lax.all_to_all(partial_value, "ctx", split_axis=0, concat_axis=0, tiled=True),
        "ep",
        split_axis=1,
        concat_axis=1,
        tiled=True,
    )
    merged = jnp.sum(
        returned.reshape(ctx_count, exp_row, SPLIT, capacity, D).astype(jnp.float32), axis=2
    ).astype(jnp.bfloat16)
    expert_rows = merged.reshape(expert_count * capacity, D)[slot_index]
    picked = expert_rows.reshape(tok_rows, TOP, D).astype(jnp.float32)
    routed_sum = jnp.sum(picked * gate_weights[:, :, None], axis=1)
    return (widened + routed_sum).astype(jnp.bfloat16)


def solution(mesh):
    return jax.shard_map(
        local,
        mesh=mesh,
        in_specs=(
            P("ctx", "ep"),
            P("ctx", None),
            P("ctx", None),
            P("ctx"),
            P("ep", "ctx"),
            P(("ctx", "ep"), None),
            P(),
            P(None, ("ctx", "ep")),
            P(None, ("ctx", "ep")),
            P(("ctx", "ep"), None),
            P(("ctx", "ep"), None),
            P(("ctx", "ep"), None),
        ),
        out_specs=P(("ctx", "ep"), None),
        check_vma=False,
    )
```

profile of v0, /device:TPU:151, one launch (start us, length us, event | category | flops | bytes accessed | tf_op | source)
XLA Modules:
  0.0 1208.3 jit_solution(10081355045997484321)
XLA Ops:
  16.2 9.0 all-reduce
  26.6 49.6 %all-gather.4.cloned.1.call-done = bf16[4096,128]{1,0:T(8,128)(2,1)} async-done(((bf16[256,128]{1,0:T(8,128)(2,1)}), bf16[4096,128]{1,0:T(8,128)(2,1)}) %all-gather.4.cloned.1.call-update) | async-done | bytes 1048592 | tf_op jit(solution)/shard_map/all_gather | solution.py:92
  76.2 81.1 %all-gather.6.cloned.1.call-done = bf16[4096,128]{1,0:T(8,128)(2,1)} async-done(((bf16[256,128]{1,0:T(8,128)(2,1)}), bf16[4096,128]{1,0:T(8,128)(2,1)}) %all-gather.6.cloned.1.call-update) | async-done | bytes 1048592 | tf_op jit(solution)/shard_map/all_gather | solution.py:93
  158.1 155.0 %while.15 = (s32[]{:T(128)}, f32[4,256]{1,0:T(4,128)S(1)}, f32[4,256]{1,0:T(4,128)S(1)}, f32[4,256,128]{2,1,0:T(8,128)}, s32[32]{0:T(128)S(1)}, /*index=5*/s32[]...) while((s32[]{:T(128)}, f32[4,256]{1,0:T(4,128)S(1)}, ...), condition=%wide.region_6.7_spmd.clone, body=%wide.region_1.6_spmd.clone.sunk | while | flops 68585856 | bytes 3153219 | solution.py:101
  316.3 4.8 convolution_convert_fusion.1
  323.8 127.3 %reduce-scatter.2.cloned.1.call-done = bf16[16,4096]{1,0:T(8,128)(2,1)} async-done(((bf16[256,4096]{1,0:T(8,128)(2,1)}), bf16[16,4096]{1,0:T(8,128)(2,1)}) %reduce-scatter.2.cloned.1.call-update) | async-done | bytes 131088 | tf_op jit(solution)/shard_map/reduce_scatter | solution.py:114
  456.7 7.1 broadcast_in_dim.66
  463.8 4.8 copy.55
  468.6 6.5 broadcast_in_dim.67
  475.1 10.2 reshape.118
  485.2 143.4 %all_to_all.20 = bf16[16,16,3,4096]{3,1,2,0:T(8,128)(2,1)S(1)} all-to-all(bf16[16,16,3,4096]{3,1,2,0:T(8,128)(2,1)} %reshape.118), channel_id=1, replica_groups=mesh['ctx'=16,'ep'=16] {'ctx'}, dimensions={0} | all-to-all | bytes 12582912 | tf_op jit(solution)/shard_map/all_to_all | solution.py:141
  632.0 150.3 %all_to_all.21 = bf16[16,16,3,4096]{3,0,2,1:T(8,128)(2,1)} all-to-all(bf16[16,16,3,4096]{3,0,2,1:T(8,128)(2,1)S(1)} %copy.56), channel_id=1, replica_groups=mesh['ctx'=16,'ep'=16] {'ep'}, dimensions={1} | all-to-all | bytes 12582912 | tf_op jit(solution)/shard_map/all_to_all | solution.py:140
  782.4 11.4 copy.57
  793.8 13.7 %reshape.119 = bf16[768,4096]{1,0:T(8,128)(2,1)} reshape(bf16[16,16,3,4096]{3,2,1,0:T(4,128)(2,1)} %copy.57) | data formatting | bytes 12582912 | tf_op jit(solution)/shard_map/reshape | solution.py:147
  807.5 8.1 fusion.34
  815.7 11.6 convolution_convert_fusion
  827.3 13.0 %reshape.120 = bf16[16,16,3,4096]{3,2,1,0:T(4,128)(2,1)} reshape(bf16[768,4096]{1,0:T(8,128)(2,1)} %convolution_convert_fusion) | data formatting | bytes 12582912 | tf_op jit(solution)/shard_map/reshape | solution.py:147
  840.3 8.5 copy.58
  848.8 140.5 %all_to_all.22 = bf16[16,16,3,4096]{3,1,2,0:T(8,128)(2,1)} all-to-all(bf16[16,16,3,4096]{3,1,2,0:T(8,128)(2,1)S(1)} %copy.58), channel_id=1, replica_groups=mesh['ctx'=16,'ep'=16] {'ctx'}, dimensions={0} | all-to-all | bytes 12582912 | tf_op jit(solution)/shard_map/all_to_all | solution.py:151
  989.2 8.9 copy.59
  998.1 12.5 %all-to-all-start.3 = ((bf16[16,16,3,4096]{3,0,2,1:T(8,128)(2,1)}), bf16[16,16,3,4096]{3,0,2,1:T(8,128)(2,1)}, u32[]{:S(2)}, u32[]{:S(2)}) async-start(bf16[16,16,3,4096]{3,0,2,1:T(8,128)(2,1)} %copy.59), calls=%async_computation.4 | async-start | bytes 12582912 | tf_op jit(solution)/shard_map/all_to_all | solution.py:150
  1010.8 165.8 %all-to-all-done.3 = bf16[16,16,3,4096]{3,0,2,1:T(8,128)(2,1)} async-done(((bf16[16,16,3,4096]{3,0,2,1:T(8,128)(2,1)}), bf16[16,16,3,4096]{3,0,2,1:T(8,128)(2,1)}, u32[]{:S(2)}, u32[]{:S(2)}) %all-to-all-start.3) | async-done | bytes 6291488 | tf_op jit(solution)/shard_map/all_to_all | solution.py:150
  1185.8 7.4 reshape.122
  1193.2 5.6 gather_fusion
  (382 shorter events, 227.3 us)
Async XLA Ops:
  6.5 809.1 %copy-start = (bf16[384,4096]{1,0:T(8,128)(2,1)S(1)}, bf16[384,4096]{1,0:T(8,128)(2,1)}, u32[]{:S(2)}) copy-start(bf16[384,4096]{1,0:T(8,128)(2,1)} %param.25) | copy-start | bytes 9437188
  6.5 69.6 %all-gather.4.cloned.1.call-start = ((), (), s32[]{:S(2)}) async-start(), calls=%async_computation.5 | async-start | bytes 1114112 | tf_op jit(solution)/shard_map/all_gather | solution.py:92
  8.2 149.1 %all-gather.6.cloned.1.call-start = ((), (), s32[]{:S(2)}) async-start(), calls=%async_computation.6 | async-start | bytes 1114112 | tf_op jit(solution)/shard_map/all_gather | solution.py:93
  9.7 306.5 %all-gather.8.cloned.1.call-start = ((), (), s32[]{:S(2)}) async-start(), calls=%async_computation.7 | async-start | bytes 4456448 | tf_op jit(solution)/shard_map/all_gather | solution.py:109
  10.5 440.7 %reduce-scatter.2.cloned.1.call-start = ((), (), s32[]{:S(2)}) async-start(), calls=%async_computation.8 | async-start | bytes 2228224 | tf_op jit(solution)/shard_map/reduce_scatter | solution.py:114
  316.3 134.9 %copy-start.2 = (bf16[16,4096]{1,0:T(8,128)(2,1)S(1)}, bf16[16,4096]{1,0:T(8,128)(2,1)}, u32[]{:S(2)}) copy-start(bf16[16,4096]{1,0:T(8,128)(2,1)} %param.21) | copy-start | bytes 393220
  316.3 136.0 %copy-start.3 = (f32[4096]{0:T(1024)S(1)}, f32[4096]{0:T(1024)}, u32[]{:S(2)}) copy-start(f32[4096]{0:T(1024)} %param.22) | copy-start | bytes 49156
  998.1 12.5 %copy-start.4 = (f32[16,8]{0,1:T(8,128)S(1)}, f32[16,8]{0,1:T(8,128)}, u32[]{:S(2)}) copy-start(f32[16,8]{0,1:T(8,128)} %param.27) | copy-start | bytes 1540
  998.1 12.6 %copy-start.5 = (s32[128]{0:T(128)S(1)}, s32[128]{0:T(128)}, u32[]{:S(2)}) copy-start(s32[128]{0:T(128)} %fusion.31) | copy-start | bytes 1540
  998.1 178.4 %all-to-all-start.3 = ((bf16[16,16,3,4096]{3,0,2,1:T(8,128)(2,1)}), bf16[16,16,3,4096]{3,0,2,1:T(8,128)(2,1)}, u32[]{:S(2)}, u32[]{:S(2)}) async-start(bf16[16,16,3,4096]{3,0,2,1:T(8,128)(2,1)} %copy.59), calls=%async_computation.4 | async-start | bytes 12582912 | tf_op jit(solution)/shard_map/all_to_all | solution.py:150
  1193.2 8.4 copy-start.1
Sparse Core Ops, SparseCore 0:
  9.1 66.9 all-gather.3
  78.0 79.2 all-gather.5
  159.0 92.4 all-gather.7
  321.3 129.8 reduce-scatter.1
where the time goes:
time: 1220 us; the launch traced here: 1210 us
  blocking collectives  443 us (36%)
  waiting for transfers between devices  424 us (35%)
  local copies, waits for them, and re-layouts  141 us (12%)
  matrix products  95.4 us (8%)
  loops' own time  58.8 us (5%)
  other arithmetic  19.2 us (2%)
  between operations  14.1 us (1%)
  starting transfers between devices  12.6 us (1%)
    all_to_all x1, waiting for transfers between devices, local(): lax.all_to_all(lax.all_to_all(partial_value, 'ctx', split_axis=0, concat_...  166 us
    all_to_all x1, blocking collectives, local(): lax.all_to_all(lax.all_to_all(packed, 'ctx', split_axis=0, concat_axis=0,...  150 us
    all_to_all x1, blocking collectives, local(): lax.all_to_all(packed, 'ctx', split_axis=0, concat_axis=0, tiled=True)  143 us
    all_to_all x1, blocking collectives, local(): lax.all_to_all(partial_value, 'ctx', split_axis=0, concat_axis=0, tiled=T...  140 us
    reduce_scatter x1, waiting for transfers between devices, local(): lax.psum_scatter(lax.optimization_barrier(group_part).astype(jnp.float32)...  127 us
    all_gather x1, waiting for transfers between devices, local(): value_piece = lax.all_gather(value_head, 'ctx', axis=0, tiled=True)  81.1 us
    all_gather x1, waiting for transfers between devices, local(): key_piece = lax.all_gather(key_head, 'ctx', axis=0, tiled=True)  49.6 us
    dot_general x22, matrix products, update(): jnp.einsum('hqk,kd->hqd', unnorm.astype(jnp.bfloat16), value_block, prefe...  48.7 us
  transfers between devices with their start and end apart: 5, of which 4 were waited for; matrix products, arithmetic and copies ran while one was open for 9% of the time, Pallas kernels for 0%

commit v1 on v0

v1 whole, which is shorter than its diff:
```python
import functools
import math

import jax
import jax.numpy as jnp
import numpy as np
from jax import lax
from jax.experimental import pallas as pl
from jax.experimental.pallas import tpu as pltpu
from jax.sharding import PartitionSpec as P

MESH = pl.DeviceIdType.MESH
BF = jnp.bfloat16
F32 = jnp.float32

D = 4096
HEAD = 128
TOP = 8
NEG = -1e30
EPS = 1e-06
SCALE = 1.0 / math.sqrt(HEAD)

NC = 4
CW = D // NC
ROWS = 16
CAP = 3
SLOT = 8 * CAP
FH = 384


def here():
    c = lax.axis_index("ctx")
    e = lax.axis_index("ep")
    return (e // 2) % 4, c % 4, e // 8, c // 4, e % 2


def device(x, y, z_hi, z_lo, core):
    return (z_lo * 4 + y, z_hi * 8 + x * 2 + core)


def remote(src, dst, send, recv, target):
    return pltpu.make_async_remote_copy(
        src_ref=src, dst_ref=dst, send_sem=send, recv_sem=recv, device_id=target, device_id_type=MESH
    )


def attend_kernel(
    q_ref, k_ref, v_ref, order_ref, proj_ref, resid_ref, gain_ref, routes_ref, gates_ref,
    normed_ref, hidden_ref, pick_ref, weigh_ref,
    kv, scores, qpos, peak, att, proj, part, other, send_x, from_x, send_z, from_z, wide,
    load_sem, zs, zr, ys, yr, cs, cr, ps, pr, as_, ar, d1s, d1r, d2s, d2r, d3s, d3r,
):
    x, y, z_hi, z_lo, core = here()
    partner = device(x, y, z_hi, z_lo, 1 - core)

    def along_z(d):
        return device(x, y, z_hi, (z_lo + d) % 4, core)

    def along_y(d):
        return device(x, (y + d) % 4, z_hi, z_lo, core)

    def along_x(d):
        return device((x + d) % 4, y, z_hi, z_lo, core)

    def along_yz(dy, dz):
        return device(x, (y + 4 - dy) % 4, (z_hi + dz) % 2, z_lo, core)

    head_col = pl.multiple_of((z_hi * 2 + x // 2) * HEAD, HEAD)
    loads = [
        pltpu.make_async_copy(k_ref.at[:, pl.ds(head_col, HEAD)], kv.at[0, 0, 0, pl.ds(0, 256), :], load_sem.at[0]),
        pltpu.make_async_copy(v_ref.at[:, pl.ds(head_col, HEAD)], kv.at[1, 0, 0, pl.ds(0, 256), :], load_sem.at[1]),
        pltpu.make_async_copy(proj_ref, proj.at[0], load_sem.at[2]),
    ]
    for c in loads:
        c.start()

    barrier = pltpu.get_barrier_semaphore()
    peers = [partner]
    peers += [along_z(d) for d in (1, 2, 3)] + [along_y(d) for d in (1, 2, 3)] + [along_x(d) for d in (1, 2, 3)]
    peers += [along_yz(dy, 1) for dy in range(4)]
    for p in peers:
        pl.semaphore_signal(barrier, inc=1, device_id=p, device_id_type=MESH)

    first = order_ref[0].astype(F32)
    second = order_ref[1].astype(F32)
    row16 = lax.broadcasted_iota(jnp.int32, (16, HEAD), 0)
    tail = jnp.where(row16 < 8, first, second).astype(BF)
    kv[0, 0, 0, 256:272, :] = tail
    kv[1, 0, 0, 256:272, :] = tail
    row = lax.broadcasted_iota(jnp.int32, (256, HEAD), 0)
    qpos[...] = jnp.where(row < 128, first * 128.0 + row.astype(F32), (second - 1.0) * 128.0 + row.astype(F32))

    loads[0].wait()
    loads[1].wait()
    pl.semaphore_wait(barrier, len(peers))

    z_copies = [remote(kv.at[core, 0, 0], kv.at[core, d, 0], zs.at[d - 1], zr.at[d - 1], along_z(d)) for d in (1, 2, 3)]
    for c in z_copies:
        c.start()

    def y_copy(d, dy):
        i = d * 3 + dy - 1
        return remote(kv.at[core, d, 0], kv.at[core, d, dy], ys.at[i], yr.at[i], along_y(dy))

    def core_copy(d, dy):
        i = d * 4 + dy
        return remote(kv.at[core, d, dy], kv.at[core, d, dy], cs.at[i], cr.at[i], partner)

    def core_arrival(d, dy):
        i = d * 4 + dy
        return remote(kv.at[1 - core, d, dy], kv.at[1 - core, d, dy], cs.at[i], cr.at[i], partner)

    for d in range(4):
        if d > 0:
            z_copies[d - 1].wait_recv()
        for dy in (1, 2, 3):
            y_copy(d, dy).start()
        if d > 0:
            core_copy(d, 0).start()
    loads[2].wait()
    p_copies = [remote(proj.at[0], proj.at[d], ps.at[d - 1], pr.at[d - 1], along_z(d)) for d in (1, 2, 3)]
    for c in p_copies:
        c.start()

    row = lax.broadcasted_iota(jnp.int32, (128, 128), 0)
    lane = lax.broadcasted_iota(jnp.int32, (128, 128), 1)
    z_to = (z_hi * 4 + z_lo + (row >> 4)) & 7
    x_to = (x + ((row >> 2) & 3)) & 3
    y_to = (y + (row & 3)) & 3
    expert = (z_to & 3) * 32 + y_to * 8 + (z_to >> 2) * 4 + x_to
    own = (lane >> 4) == (row >> 4)
    named = jnp.zeros((128, 128), F32)
    weight = jnp.zeros((128, 128), F32)
    for j in range(TOP):
        hit = jnp.where(own & (routes_ref[j : j + 1, :] == expert), 1.0, 0.0)
        named = named + hit
        weight = weight + hit * gates_ref[j : j + 1, :]
    before = jnp.where(row < lane, 1.0, 0.0).astype(BF)
    rank = jnp.dot(named.astype(BF), before, preferred_element_type=F32)
    for r in range(CAP):
        at = jnp.where((named > 0.5) & (jnp.abs(rank - r) < 0.5), 1.0, 0.0)
        pick_ref[:, r] = at.reshape(8, 16, 128).astype(BF)
        weigh_ref[:, r] = (at * weight).reshape(8, 16, 128).astype(BF)

    for d in range(4):
        for dy in (1, 2, 3):
            y_copy(d, dy).wait_recv()
            core_copy(d, dy).start()
    for d in range(4):
        for dy in range(4):
            if d + dy > 0:
                core_arrival(d, dy).wait_recv()

    lanes = lax.broadcasted_iota(jnp.int32, (8, HEAD), 1).astype(F32)

    def one_head(h, _):
        cols = pl.ds(pl.multiple_of(h * HEAD, HEAD), HEAD)
        query = q_ref[:, cols]

        def score(s, top):
            d, dy = s // 4, s % 4
            keys = kv[0, d, dy, 0:256, :]
            ids = kv[0, d, dy, 256:272, :].astype(F32) * 128.0
            got = lax.dot_general(query, keys, (((1,), (1,)), ((), ())), preferred_element_type=F32)
            at_first = (ids[0:8] + lanes)[0:1]
            at_second = (ids[8:16] + lanes)[0:1]
            left = jnp.where(at_first <= qpos[...], got[:, :HEAD], NEG)
            right = jnp.where(at_second <= qpos[...], got[:, HEAD:], NEG)
            scores[s, :, 0:HEAD] = left
            scores[s, :, HEAD:256] = right
            return jnp.maximum(top, jnp.maximum(left, right))

        top = lax.fori_loop(0, 16, score, jnp.full((256, HEAD), NEG, F32))
        peak[...] = jnp.broadcast_to(jnp.max(top, axis=1, keepdims=True), (256, HEAD))

        def gather(s, carried):
            total, acc = carried
            d, dy = s // 4, s % 4
            left = jnp.exp((scores[s, :, 0:HEAD] - peak[...]) * SCALE)
            right = jnp.exp((scores[s, :, HEAD:256] - peak[...]) * SCALE)
            both = jnp.concatenate([left.astype(BF), right.astype(BF)], axis=1)
            acc = acc + jnp.dot(both, kv[1, d, dy, 0:256, :], preferred_element_type=F32)
            return total + (left + right), acc

        zero = jnp.zeros((256, HEAD), F32)
        total, acc = lax.fori_loop(0, 16, gather, (zero, zero))
        att[0, :, cols] = (acc / jnp.sum(total, axis=1, keepdims=True)).astype(BF)
        for dy in (1, 2, 3):
            remote(att.at[0, :, cols], att.at[dy, :, cols], as_.at[dy - 1], ar.at[dy - 1], along_y(dy)).start()
        return 0

    lax.fori_loop(0, 4, one_head, 0)

    for c in p_copies:
        c.wait_recv()

    def att_copy(dy):
        return remote(att.at[0], att.at[dy], as_.at[dy - 1], ar.at[dy - 1], along_y(dy))

    def core_part(dy):
        return remote(part.at[dy, 1 - core], other.at[dy], d1s.at[dy], d1r.at[dy], partner)

    for dy in range(4):
        if dy > 0:
            att_copy(dy).wait_recv()

        def project(d, _):
            got = jnp.dot(att[dy], proj[d], preferred_element_type=F32).astype(BF)
            got = got.reshape(2, 4, 2, ROWS, 256)
            cols = pl.ds(pl.multiple_of(d * 256, 256), 256)
            part[dy, 0, :, :, :, cols] = got[:, :, 0]
            part[dy, 1, :, :, :, cols] = got[:, :, 1]
            return 0

        lax.fori_loop(0, 4, project, 0)
        core_part(dy).start()

    def x_copy(dy, dx):
        i = dy * 3 + dx - 1
        return remote(send_x.at[dy, dx], from_x.at[dy, dx - 1], d2s.at[i], d2r.at[i], along_x(dx))

    for dy in range(4):
        core_part(dy).wait_recv()
        for dx in (1, 2, 3, 0):
            x_to = (x + dx) % 4
            for dz in range(2):
                z_to = (z_hi + dz) % 2
                mine = part[dy, core, z_to, x_to].astype(F32) + other[dy, z_to, x_to].astype(F32)
                send_x[dy, dx, dz] = mine.astype(BF)
            if dx > 0:
                x_copy(dy, dx).start()

    def yz_copy(dy, dz):
        i = dy * 2 + dz
        return remote(send_z.at[dy, dz], from_z.at[dy, dz], d3s.at[i], d3r.at[i], along_yz(dy, dz))

    for dy in range(4):
        for dx in (1, 2, 3):
            x_copy(dy, dx).wait_recv()
        for dz in (1, 0):
            got = send_x[dy, 0, dz].astype(F32) + from_x[dy, 0, dz].astype(F32)
            got = got + (from_x[dy, 1, dz].astype(F32) + from_x[dy, 2, dz].astype(F32))
            if dy + dz > 0:
                send_z[dy, dz] = got.astype(BF)
                yz_copy(dy, dz).start()
            else:
                from_z[0, 0] = got.astype(BF)

    square = jnp.zeros((ROWS, 256), F32)
    for dy in range(4):
        for dz in range(2):
            if dy + dz > 0:
                yz_copy(dy, dz).wait_recv()
        for d in range(4):
            col = (((z_lo + 4 - d) % 4) * 4 + (y + dy) % 4) * 256
            cols = pl.ds(pl.multiple_of(col, 256), 256)
            got = from_z[dy, 0, :, d * 256 : d * 256 + 256].astype(F32) + from_z[dy, 1, :, d * 256 : d * 256 + 256].astype(F32)
            state = (resid_ref[:, cols].astype(F32) + got).astype(BF)
            hidden_ref[:, cols] = state
            state = state.astype(F32)
            wide[:, cols] = state
            square = square + state * state
    mean = jnp.sum(square, axis=1, keepdims=True) * (1.0 / D)
    normed_ref[...] = (wide[...] * lax.rsqrt(mean + EPS) * gain_ref[...]).astype(BF)

    for c in z_copies + p_copies:
        c.wait_send()
    for d in range(4):
        for dy in (1, 2, 3):
            y_copy(d, dy).wait_send()
        for dy in range(4):
            if d + dy > 0:
                core_copy(d, dy).wait_send()
    for dy in range(4):
        if dy > 0:
            att_copy(dy).wait_send()
        core_part(dy).wait_send()
        for dx in (1, 2, 3):
            x_copy(dy, dx).wait_send()
        for dz in range(2):
            if dy + dz > 0:
                yz_copy(dy, dz).wait_send()


def expert_kernel(
    normed_ref, hidden_ref, pick_ref, weigh_ref, perm_ref, wg_ref, wu_ref, wd_ref,
    out_ref,
    wg, wu, wd, pick, weigh, choose, spread, tok, packed, rows, acc_g, acc_u, act, back, ret, summed, from_z,
    lg, lu, ld, gs, gr, us, ur, ws, wr, os_, or_, ts, tr, xs, xr, rs, rr, fs, fr,
):
    x, y, z_hi, z_lo, core = here()
    z = z_hi * 4 + z_lo
    partner = device(x, y, z_hi, z_lo, 1 - core)

    def along_z(d):
        to = (z + d) % 8
        return device(x, y, to // 4, to % 4, core)

    def in_plane(i):
        return device((x + i // 4) % 4, (y + i % 4) % 4, z_hi, z_lo, core)

    def plane_back(i):
        return device((x + 4 - i // 4) % 4, (y + 4 - i % 4) % 4, z_hi, z_lo, core)

    def chunk(j):
        return pl.ds(pl.multiple_of(j * CW, CW), CW)

    own_half = pl.ds(0, FH)
    far_half = pl.ds(FH, FH)

    def local_g(j):
        return pltpu.make_async_copy(wg_ref.at[chunk(j), :], wg.at[chunk(j), own_half], lg.at[j])

    def local_u(j):
        return pltpu.make_async_copy(wu_ref.at[chunk(j), :], wu.at[chunk(j), own_half], lu.at[j])

    def far_g(j):
        return remote(wg_ref.at[chunk(j), :], wg.at[chunk(j), far_half], gs.at[j], gr.at[j], partner)

    def far_u(j):
        return remote(wu_ref.at[chunk(j), :], wu.at[chunk(j), far_half], us.at[j], ur.at[j], partner)

    local_d = pltpu.make_async_copy(wd_ref, wd.at[own_half, :], ld.at[0])
    far_d = remote(wd_ref, wd.at[far_half, :], ws.at[0], wr.at[0], partner)

    barrier = pltpu.get_barrier_semaphore()
    pl.semaphore_signal(barrier, inc=1, device_id=partner, device_id_type=MESH)

    def greet_z(d, _):
        pl.semaphore_signal(barrier, inc=1, device_id=along_z(d), device_id_type=MESH)
        return 0

    def greet_plane(i, _):
        pl.semaphore_signal(barrier, inc=1, device_id=in_plane(i), device_id_type=MESH)
        return 0

    lax.fori_loop(1, 8, greet_z, 0)
    lax.fori_loop(1, 16, greet_plane, 0)

    for j in range(NC):
        tok[j, 0] = normed_ref[:, j * CW : (j + 1) * CW]
    pick[0] = pick_ref[0]
    weigh[0] = weigh_ref[0]

    pl.semaphore_wait(barrier, 23)

    def send_picks(d, _):
        remote(pick_ref.at[d], pick.at[d], os_.at[0], or_.at[0], along_z(d)).start()
        remote(weigh_ref.at[d], weigh.at[d], os_.at[1], or_.at[1], along_z(d)).start()
        return 0

    def all_picks():
        return (
            remote(pick_ref.at[pl.ds(1, 7)], pick.at[pl.ds(1, 7)], os_.at[0], or_.at[0], partner),
            remote(weigh_ref.at[pl.ds(1, 7)], weigh.at[pl.ds(1, 7)], os_.at[1], or_.at[1], partner),
        )

    def send_tokens(j, _):
        def one(d, _):
            remote(tok.at[j, 0], tok.at[j, d], ts.at[j], tr.at[j], along_z(d)).start()
            return 0

        lax.fori_loop(1, 8, one, 0)
        return 0

    lax.fori_loop(1, 8, send_picks, 0)
    lax.fori_loop(0, NC, send_tokens, 0)
    for j in range(NC):
        local_g(j).start()
        local_u(j).start()
        far_g(j).start()
        far_u(j).start()
    local_d.start()
    far_d.start()

    acc_g[...] = jnp.zeros_like(acc_g)
    acc_u[...] = jnp.zeros_like(acc_u)

    for c in all_picks():
        c.wait_recv()
    perm = perm_ref[...]
    choose[...] = jnp.dot(perm, pick[...].reshape(16 * SLOT, 128), preferred_element_type=F32).astype(BF)
    spread[...] = jnp.dot(perm, weigh[...].reshape(16 * SLOT, 128), preferred_element_type=F32).T.astype(BF)

    def all_tokens(j):
        return remote(tok.at[j, pl.ds(1, 7)], tok.at[j, pl.ds(1, 7)], ts.at[j], tr.at[j], partner)

    def all_rows(j):
        return remote(packed.at[j], rows.at[j, pl.ds(1, 15)], xs.at[j], xr.at[j], partner)

    def all_back(j):
        return remote(back.at[j], ret.at[j, pl.ds(1, 15)], rs.at[j], rr.at[j], partner)

    def all_sums(j):
        return remote(summed.at[j, pl.ds(1, 7)], from_z.at[j, pl.ds(1, 7)], fs.at[j], fr.at[j], partner)

    def pack(j, _):
        all_tokens(j).wait_recv()

        def columns(n, _):
            cols = pl.ds(pl.multiple_of(n * 256, 256), 256)
            got = jnp.dot(choose[...], tok[j, :, :, cols].reshape(128, 256), preferred_element_type=F32)
            got = got.astype(BF).reshape(16, SLOT, 256)
            rows[j, 0, :, cols] = got[0]
            packed[j, :, :, cols] = got[1:]
            return 0

        lax.fori_loop(0, CW // 256, columns, 0)

        def send(i, _):
            remote(packed.at[j, i - 1], rows.at[j, i], xs.at[j], xr.at[j], in_plane(i)).start()
            return 0

        lax.fori_loop(1, 16, send, 0)
        return 0

    lax.fori_loop(0, NC, pack, 0)

    def upward(j, _):
        local_g(j).wait()
        local_u(j).wait()
        far_g(j).wait_recv()
        far_u(j).wait_recv()
        all_rows(j).wait_recv()

        def columns(n, _):
            cols = pl.ds(pl.multiple_of(n * 256, 256), 256)
            got = rows[j].reshape(16 * SLOT, CW)
            acc_g[:, cols] += jnp.dot(got, wg[chunk(j), cols], preferred_element_type=F32)
            acc_u[:, cols] += jnp.dot(got, wu[chunk(j), cols], preferred_element_type=F32)
            return 0

        lax.fori_loop(0, 3, columns, 0)
        return 0

    lax.fori_loop(0, NC, upward, 0)
    act[...] = (jax.nn.silu(acc_g[...]) * acc_u[...]).astype(BF)
    local_d.wait()
    far_d.wait_recv()

    def downward(j, _):
        def columns(n, _):
            cols = pl.ds(pl.multiple_of(n * 256, 256), 256)
            far = pl.ds(pl.multiple_of(j * CW + n * 256, 256), 256)
            got = jnp.dot(act[...], wd[:, far], preferred_element_type=F32).astype(BF).reshape(16, SLOT, 256)
            ret[j, 0, :, cols] = got[0]
            back[j, :, :, cols] = got[1:]
            return 0

        lax.fori_loop(0, CW // 256, columns, 0)

        def send(i, _):
            remote(back.at[j, i - 1], ret.at[j, i], rs.at[j], rr.at[j], plane_back(i)).start()
            return 0

        lax.fori_loop(1, 16, send, 0)
        return 0

    lax.fori_loop(0, NC, downward, 0)

    def combine(j, _):
        all_back(j).wait_recv()

        def columns(n, _):
            cols = pl.ds(pl.multiple_of(n * 256, 256), 256)
            got = ret[j, :, :, cols].reshape(16 * SLOT, 256)
            got = jnp.dot(spread[...], got, preferred_element_type=F32)
            summed[j, :, :, cols] = got.astype(BF).reshape(8, ROWS, 256)
            return 0

        lax.fori_loop(0, CW // 256, columns, 0)

        def send(d, _):
            remote(summed.at[j, d], from_z.at[j, d], fs.at[j], fr.at[j], along_z(8 - d)).start()
            return 0

        lax.fori_loop(1, 8, send, 0)
        return 0

    lax.fori_loop(0, NC, combine, 0)

    def finish(j, _):
        all_sums(j).wait_recv()
        total = summed[j, 0].astype(F32)
        for d in range(1, 8):
            total = total + from_z[j, d].astype(F32)
        out_ref[:, chunk(j)] = (hidden_ref[:, chunk(j)].astype(F32) + total).astype(BF)
        return 0

    lax.fori_loop(0, NC, finish, 0)

    for c in all_picks():
        c.wait_send()

    def drain(j, _):
        far_g(j).wait_send()
        far_u(j).wait_send()
        all_tokens(j).wait_send()
        all_rows(j).wait_send()
        all_back(j).wait_send()
        all_sums(j).wait_send()
        return 0

    lax.fori_loop(0, NC, drain, 0)
    far_d.wait_send()


def slot_order():
    perm = np.zeros((16 * SLOT, 16 * SLOT), np.float32)
    for p in range(16):
        for s in range(8):
            for r in range(CAP):
                perm[p * SLOT + s * CAP + r, s * 16 * CAP + r * 16 + p] = 1.0
    return perm


VMEM = pl.BlockSpec(memory_space=pltpu.VMEM)
SMEM = pl.BlockSpec(memory_space=pltpu.SMEM)
ANY = pl.BlockSpec(memory_space=pl.ANY)
SHAPE = jax.ShapeDtypeStruct
DMA = pltpu.SemaphoreType.DMA


def attend(q, k, v, order, proj, resid, gain, routes, gates):
    return pl.pallas_call(
        attend_kernel,
        out_shape=(
            SHAPE((ROWS, D), BF),
            SHAPE((ROWS, D), BF),
            SHAPE((8, CAP, 16, 128), BF),
            SHAPE((8, CAP, 16, 128), BF),
        ),
        in_specs=[VMEM, ANY, ANY, SMEM, ANY, VMEM, VMEM, VMEM, VMEM],
        out_specs=(VMEM,) * 4,
        scratch_shapes=[
            pltpu.VMEM((2, 4, 4, 272, HEAD), BF),
            pltpu.VMEM((16, 256, 256), F32),
            pltpu.VMEM((256, HEAD), F32),
            pltpu.VMEM((256, HEAD), F32),
            pltpu.VMEM((4, 256, 512), BF),
            pltpu.VMEM((4, 512, 256), BF),
            pltpu.VMEM((4, 2, 2, 4, ROWS, 1024), BF),
            pltpu.VMEM((4, 2, 4, ROWS, 1024), BF),
            pltpu.VMEM((4, 4, 2, ROWS, 1024), BF),
            pltpu.VMEM((4, 3, 2, ROWS, 1024), BF),
            pltpu.VMEM((4, 2, ROWS, 1024), BF),
            pltpu.VMEM((4, 2, ROWS, 1024), BF),
            pltpu.VMEM((ROWS, D), F32),
            DMA((3,)),
            DMA((3,)), DMA((3,)),
            DMA((12,)), DMA((12,)),
            DMA((16,)), DMA((16,)),
            DMA((3,)), DMA((3,)),
            DMA((3,)), DMA((3,)),
            DMA((4,)), DMA((4,)),
            DMA((12,)), DMA((12,)),
            DMA((8,)), DMA((8,)),
        ],
        compiler_params=pltpu.CompilerParams(
            collective_id=0, has_side_effects=True, vmem_limit_bytes=48 * 1024 * 1024
        ),
        name="attend",
    )(q, k, v, order, proj, resid, gain, routes, gates)


def route_and_expert(normed, hidden, pick, weigh, perm, wg, wu, wd):
    return pl.pallas_call(
        expert_kernel,
        out_shape=SHAPE((ROWS, D), BF),
        in_specs=[VMEM, VMEM, VMEM, VMEM, VMEM, ANY, ANY, ANY],
        out_specs=VMEM,
        scratch_shapes=[
            pltpu.VMEM((D, 2 * FH), BF),
            pltpu.VMEM((D, 2 * FH), BF),
            pltpu.VMEM((2 * FH, D), BF),
            pltpu.VMEM((8, CAP, 16, 128), BF),
            pltpu.VMEM((8, CAP, 16, 128), BF),
            pltpu.VMEM((16 * SLOT, 128), BF),
            pltpu.VMEM((128, 16 * SLOT), BF),
            pltpu.VMEM((NC, 8, ROWS, CW), BF),
            pltpu.VMEM((NC, 15, SLOT, CW), BF),
            pltpu.VMEM((NC, 16, SLOT, CW), BF),
            pltpu.VMEM((16 * SLOT, 2 * FH), F32),
            pltpu.VMEM((16 * SLOT, 2 * FH), F32),
            pltpu.VMEM((16 * SLOT, 2 * FH), BF),
            pltpu.VMEM((NC, 15, SLOT, CW), BF),
            pltpu.VMEM((NC, 16, SLOT, CW), BF),
            pltpu.VMEM((NC, 8, ROWS, CW), BF),
            pltpu.VMEM((NC, 8, ROWS, CW), BF),
            DMA((NC,)), DMA((NC,)), DMA((1,)),
            DMA((NC,)), DMA((NC,)), DMA((NC,)), DMA((NC,)), DMA((1,)), DMA((1,)),
            DMA((2,)), DMA((2,)),
            DMA((NC,)), DMA((NC,)),
            DMA((NC,)), DMA((NC,)),
            DMA((NC,)), DMA((NC,)),
            DMA((NC,)), DMA((NC,)),
        ],
        compiler_params=pltpu.CompilerParams(
            collective_id=1, has_side_effects=True, vmem_limit_bytes=58 * 1024 * 1024
        ),
        name="experts",
    )(normed, hidden, pick, weigh, perm, wg, wu, wd)


def local(
    queries,
    key_states,
    value_head_states,
    block_order,
    out_proj,
    residual,
    norm_gain,
    w_gate,
    w_up,
    w_down,
    routes,
    gate_weights,
):
    routes_row = jnp.tile(routes.T, (1, 8))
    gates_row = jnp.tile(gate_weights.T, (1, 8))
    normed, hidden, pick, weigh = attend(
        queries, key_states, value_head_states, block_order, out_proj, residual,
        norm_gain.reshape(1, D), routes_row, gates_row,
    )
    perm = jnp.asarray(slot_order(), BF)
    return route_and_expert(normed, hidden, pick, weigh, perm, w_gate, w_up, w_down)


def solution(mesh):
    return jax.shard_map(
        local,
        mesh=mesh,
        in_specs=(
            P("ctx", "ep"),
            P("ctx", None),
            P("ctx", None),
            P("ctx"),
            P("ep", "ctx"),
            P(("ctx", "ep"), None),
            P(),
            P(None, ("ctx", "ep")),
            P(None, ("ctx", "ep")),
            P(("ctx", "ep"), None),
            P(("ctx", "ep"), None),
            P(("ctx", "ep"), None),
        ),
        out_specs=P(("ctx", "ep"), None),
        check_vma=False,
    )
```

time: 1220 us -> 201 us (0.16)
  the two profiles are of different devices: /device:TPU:151 before, /device:TPU:2 now
where the time goes in v1:
time: 201 us
  Pallas kernels  189 us (94%)
  local copies, waits for them, and re-layouts  11.7 us (6%)
    pallas_call x1, Pallas kernels, route_and_expert(): pl.pallas_call(expert_kernel, out_shape=SHAPE((ROWS, D), BF), in_specs=[V...  111 us
    pallas_call x1, Pallas kernels, attend(): pl.pallas_call(attend_kernel, out_shape=(SHAPE((ROWS, D), BF), SHAPE((ROW...  78.3 us
    unnamed x23, local copies, waits for them, and re-layouts  10.2 us

profile of v1, /device:TPU:2, one launch (start us, length us, event | category | flops | bytes accessed | tf_op | source)
XLA Modules:
  0.0 201.0 jit_solution(7421659771995391468)
XLA Ops:
  0.0 0.7 tile.8
  0.7 0.1 tile.9.routes_ref
  0.8 0.7 tile.20
  1.5 0.1 tile.21.gates_ref
  1.5 0.0 copy-start
  1.5 0.9 copy-done
  2.5 0.0 copy-start.1
  2.5 0.9 copy-done.1
  3.4 0.0 copy-start.2
  3.4 0.9 copy-done.2
  4.4 0.0 copy-start.3
  4.4 0.9 copy-done.3
  5.3 0.0 copy-start.6
  5.3 0.9 copy-done.6
  6.2 0.7 copy-done.9
  7.0 0.7 copy-done.10
  7.6 78.3 %attend.1 = (bf16[16,4096]{1,0:T(8,128)(2,1)S(1)}, bf16[16,4096]{1,0:T(8,128)(2,1)S(1)}, bf16[8,3,16,128]{3,2,1,0:T(8,128)(2,1)S(1)}, bf16[8,3,16,128]{3,2,1,0:T(8,128)(2,1)S(1)}) custom-call(bf16[256,512]{1,0:T(8,128)(2,1)S(1)} %copy-done, bf16[256,512]{1,0:T(8,128)(2,1)S(1)} %copy-done.1, bf16[256,512]{1,0:T(8,128)(2,1)S(1)} %copy-done.2, ...), custom_call_target="tpu_custom_call" | custom-call | tf_op jit(solution)/shard_map/attend/pallas_call | solution.py:525
  85.9 0.0 copy-start.4
  85.9 0.6 copy-done.4
  86.6 0.6 copy-done.5
  87.2 0.6 copy-done.7
  87.8 0.6 copy-done.8
  88.5 111.0 %experts.1 = bf16[16,4096]{1,0:T(8,128)(2,1)} custom-call(bf16[16,4096]{1,0:T(8,128)(2,1)} %copy-done.4, bf16[16,4096]{1,0:T(8,128)(2,1)} %copy-done.5, bf16[8,3,16,128]{3,2,1,0:T(8,128)(2,1)} %copy-done.7, bf16[8,3,16,128]{3,2,1,0:T(8,128)(2,1)} %copy-done.8, bf16[384,384]{1,0:T(8,128)(2,1)} %constant.2.clone.perm_ref, bf16[4096,384]{1,0:T(8,128)(2,1)} %wg_ref.1, ...), custom_call_target="tpu_custom_call" | custom-call | tf_op jit(solution)/shard_map/experts/pallas_call | solution.py:567
  199.5 1.6 copy.15
  (5 shorter events, 0.0 us)
Async XLA Ops:
  1.5 1.0 copy-start
  2.5 0.9 copy-start.1
  3.4 0.9 copy-start.2
  4.4 0.9 copy-start.3
  5.3 0.9 copy-start.6
  6.2 0.7 copy-start.9
  7.0 0.7 copy-start.10
  85.9 0.7 copy-start.4
  86.6 0.6 copy-start.5
  87.2 0.6 copy-start.7
  87.8 0.6 copy-start.8

commit v2 on v0

v2 whole, which is shorter than its diff:
```python
import math

import jax
import jax.numpy as jnp
import numpy as np
from jax import lax
from jax.experimental import pallas as pl
from jax.experimental.pallas import tpu as pltpu
from jax.sharding import PartitionSpec as P

MESH = pl.DeviceIdType.MESH
BF = jnp.bfloat16
F32 = jnp.float32

D = 4096
HEAD = 128
TOP = 8
NEG = -1e30
EPS = 1e-06
SCALE = 1.0 / math.sqrt(HEAD)

SUB = 2
NC = 4 * SUB
CW = D // NC
ROWS = 16
CAP = 3
SLOT = 8 * CAP
SLOTS = 16 * SLOT
FH = 384


def here():
    c = lax.axis_index("ctx")
    e = lax.axis_index("ep")
    return (e // 2) % 4, c % 4, e // 8, c // 4, e % 2


def device(x, y, z_hi, z_lo, core):
    return (z_lo * 4 + y, z_hi * 8 + x * 2 + core)


def remote(src, dst, send, recv, target):
    return pltpu.make_async_remote_copy(
        src_ref=src, dst_ref=dst, send_sem=send, recv_sem=recv, device_id=target, device_id_type=MESH
    )


def layer_kernel(
    order_ref, q_hbm, k_hbm, v_hbm, proj_hbm, resid_hbm, gain_hbm, routes_hbm, perm_hbm, wg_hbm, wu_hbm, wd_hbm,
    out_ref,
    query, resid, gain, routing, perm,
    kv, scores, qpos, peak, total, acc, att, proj, part, other, send_x, from_x, send_z, from_z, hidden,
    wg, wu, wd, pick, weigh, pick_in, weigh_in, choose, spread,
    tok, scale, packed, rows, scale_out, scale_in, acc_g, acc_u, act, back, ret, summed, sums_in,
    load_sem, zs, zr, ys, yr, cs, cr, ps, pr, as_, ar, d1s, d1r, d2s, d2r, d3s, d3r,
    lg, lu, ld, gs, gr, us, ur, ws, wr, os_, or_, ts, tr, ss, sr, xs, xr, rs, rr, fs, fr,
):
    x, y, z_hi, z_lo, core = here()
    z = z_hi * 4 + z_lo
    partner = device(x, y, z_hi, z_lo, 1 - core)

    def in_span(d):
        return device(x, y, z_hi, (z_lo + d) % 4, core)

    def along_y(d):
        return device(x, (y + d) % 4, z_hi, z_lo, core)

    def along_x(d):
        return device((x + d) % 4, y, z_hi, z_lo, core)

    def along_yz(dy, dz):
        return device(x, (y + 4 - dy) % 4, (z_hi + dz) % 2, z_lo, core)

    def along_z(d):
        to = (z + d) % 8
        return device(x, y, to // 4, to % 4, core)

    def in_plane(i):
        return device((x + i // 4) % 4, (y + i % 4) % 4, z_hi, z_lo, core)

    def plane_back(i):
        return device((x + 4 - i // 4) % 4, (y + 4 - i % 4) % 4, z_hi, z_lo, core)

    def chunk(c):
        return pl.ds(pl.multiple_of(c * CW, CW), CW)

    def tile(n):
        return pl.ds(pl.multiple_of(n * 256, 256), 256)

    head_col = pl.multiple_of((z_hi * 2 + x // 2) * HEAD, HEAD)
    loads = [
        pltpu.make_async_copy(src, dst, load_sem.at[i])
        for i, (src, dst) in enumerate([
            (k_hbm.at[:, pl.ds(head_col, HEAD)], kv.at[0, 0, 0, pl.ds(0, 256), :]),
            (v_hbm.at[:, pl.ds(head_col, HEAD)], kv.at[1, 0, 0, pl.ds(0, 256), :]),
            (proj_hbm, proj.at[0]),
            (q_hbm, query),
            (routes_hbm, routing),
            (perm_hbm, perm),
            (resid_hbm, resid),
            (gain_hbm, gain),
        ])
    ]
    for c in loads:
        c.start()

    barrier = pltpu.get_barrier_semaphore()

    def greet(target):
        pl.semaphore_signal(barrier, inc=1, device_id=target, device_id_type=MESH)

    def greet_z(d, _):
        greet(along_z(d))
        return 0

    def greet_plane(i, _):
        greet(in_plane(i))
        return 0

    greet(partner)
    lax.fori_loop(1, 8, greet_z, 0)
    lax.fori_loop(1, 16, greet_plane, 0)
    for dy in (1, 2, 3):
        greet(along_yz(dy, 1))

    first = order_ref[0].astype(F32)
    second = order_ref[1].astype(F32)
    row16 = lax.broadcasted_iota(jnp.int32, (16, HEAD), 0)
    tail = jnp.where(row16 < 8, first, second).astype(BF)
    kv[0, 0, 0, 256:272, :] = tail
    kv[1, 0, 0, 256:272, :] = tail
    row = lax.broadcasted_iota(jnp.int32, (256, HEAD), 0)
    qpos[...] = jnp.where(row < 128, first * 128.0 + row.astype(F32), (second - 1.0) * 128.0 + row.astype(F32))

    loads[0].wait()
    loads[1].wait()
    pl.semaphore_wait(barrier, 26)

    def z_copy(d):
        return remote(kv.at[core, 0, 0], kv.at[core, d, 0], zs.at[d - 1], zr.at[d - 1], in_span(d))

    def y_copy(d, dy):
        i = d * 3 + dy - 1
        return remote(kv.at[core, d, 0], kv.at[core, d, dy], ys.at[i], yr.at[i], along_y(dy))

    def core_copy(d, dy):
        i = d * 4 + dy
        return remote(kv.at[core, d, dy], kv.at[core, d, dy], cs.at[i], cr.at[i], partner)

    def core_arrival(d, dy):
        i = d * 4 + dy
        return remote(kv.at[1 - core, d, dy], kv.at[1 - core, d, dy], cs.at[i], cr.at[i], partner)

    def proj_copy(d):
        return remote(proj.at[0], proj.at[d], ps.at[d - 1], pr.at[d - 1], in_span(d))

    for d in (1, 2, 3):
        z_copy(d).start()
    for dy in (1, 2, 3):
        y_copy(0, dy).start()

    loads[4].wait()
    row = lax.broadcasted_iota(jnp.int32, (128, 128), 0)
    lane = lax.broadcasted_iota(jnp.int32, (128, 128), 1)
    z_to = (z + (row >> 4)) & 7
    x_to = (x + ((row >> 2) & 3)) & 3
    y_to = (y + (row & 3)) & 3
    expert = ((z_to & 3) * 32 + y_to * 8 + (z_to >> 2) * 4 + x_to).astype(F32)
    own = (lane >> 4) == (row >> 4)
    named = jnp.zeros((128, 128), F32)
    weight = jnp.zeros((128, 128), F32)
    for j in range(TOP):
        hit = jnp.where(own & (jnp.abs(routing[j : j + 1, :] - expert) < 0.5), 1.0, 0.0)
        named = named + hit
        weight = weight + hit * routing[TOP + j : TOP + j + 1, :]
    before = jnp.where(row < lane, 1.0, 0.0).astype(BF)
    rank = jnp.dot(named.astype(BF), before, preferred_element_type=F32)
    for r in range(CAP):
        at = jnp.where((named > 0.5) & (jnp.abs(rank - r) < 0.5), 1.0, 0.0)
        pick[:, r] = at.reshape(8, 16, 128).astype(BF)
        weigh[:, r] = (at * weight).reshape(8, 16, 128).astype(BF)

    for d in (1, 2, 3):
        z_copy(d).wait_recv()
        for dy in (1, 2, 3):
            y_copy(d, dy).start()
        core_copy(d, 0).start()
    loads[2].wait()
    for d in (1, 2, 3):
        proj_copy(d).start()

    def send_picks(d, _):
        remote(pick.at[d], pick_in.at[d], os_.at[0], or_.at[0], along_z(d)).start()
        remote(weigh.at[d], weigh_in.at[d], os_.at[1], or_.at[1], along_z(d)).start()
        return 0

    lax.fori_loop(1, 8, send_picks, 0)
    pick_in[0] = pick[0]
    weigh_in[0] = weigh[0]

    own_half = pl.ds(0, FH)
    far_half = pl.ds(FH, FH)

    def local_g(c):
        return pltpu.make_async_copy(wg_hbm.at[chunk(c), :], wg.at[chunk(c), own_half], lg.at[c])

    def local_u(c):
        return pltpu.make_async_copy(wu_hbm.at[chunk(c), :], wu.at[chunk(c), own_half], lu.at[c])

    def far_g(c):
        return remote(wg_hbm.at[chunk(c), :], wg.at[chunk(c), far_half], gs.at[c], gr.at[c], partner)

    def far_u(c):
        return remote(wu_hbm.at[chunk(c), :], wu.at[chunk(c), far_half], us.at[c], ur.at[c], partner)

    local_d = pltpu.make_async_copy(wd_hbm, wd.at[own_half, :], ld.at[0])
    far_d = remote(wd_hbm, wd.at[far_half, :], ws.at[0], wr.at[0], partner)

    def start_local(c, _):
        local_g(c).start()
        local_u(c).start()
        return 0

    def start_far(c, _):
        far_g(c).start()
        far_u(c).start()
        return 0

    lanes = lax.broadcasted_iota(jnp.int32, (8, HEAD), 1).astype(F32)
    loads[3].wait()

    def group(d, last):
        for dy in range(4):
            if d + dy > 0:
                core_arrival(d, dy).wait_recv()

        def one_head(h, _):
            cols = pl.ds(pl.multiple_of(h * HEAD, HEAD), HEAD)
            q = query[:, cols]
            top = None
            for dy in range(4):
                ids = kv[0, d, dy, 256:272, :].astype(F32) * 128.0
                got = lax.dot_general(
                    q, kv[0, d, dy, 0:256, :], (((1,), (1,)), ((), ())), preferred_element_type=F32
                )
                left = jnp.where((ids[0:8] + lanes)[0:1] <= qpos[...], got[:, :HEAD], NEG)
                right = jnp.where((ids[8:16] + lanes)[0:1] <= qpos[...], got[:, HEAD:], NEG)
                scores[dy, :, 0:HEAD] = left
                scores[dy, :, HEAD:256] = right
                both = jnp.maximum(left, right)
                top = both if top is None else jnp.maximum(top, both)
            now = jnp.broadcast_to(jnp.max(top, axis=1, keepdims=True), (256, HEAD))
            if d > 0:
                old = peak[h]
                now = jnp.maximum(now, old)
                shrink = jnp.exp((old - now) * SCALE)
                sums = total[h] * shrink
                out = acc[h] * shrink
            else:
                sums = jnp.zeros((256, HEAD), F32)
                out = jnp.zeros((256, HEAD), F32)
            peak[h] = now
            for dy in range(4):
                left = jnp.exp((scores[dy, :, 0:HEAD] - peak[h]) * SCALE)
                right = jnp.exp((scores[dy, :, HEAD:256] - peak[h]) * SCALE)
                both = jnp.concatenate([left.astype(BF), right.astype(BF)], axis=1)
                out = out + jnp.dot(both, kv[1, d, dy, 0:256, :], preferred_element_type=F32)
                sums = sums + (left + right)
            if last:
                att[0, :, cols] = (out / jnp.sum(sums, axis=1, keepdims=True)).astype(BF)
                for dy in (1, 2, 3):
                    remote(att.at[0, :, cols], att.at[dy, :, cols], as_.at[dy - 1], ar.at[dy - 1], along_y(dy)).start()
            else:
                total[h] = sums
                acc[h] = out
            return 0

        lax.fori_loop(0, 4, one_head, 0)

    for d in range(4):
        for dy in (1, 2, 3):
            y_copy(d, dy).wait_recv()
            core_copy(d, dy).start()
        if d == 0:
            lax.fori_loop(0, NC, start_local, 0)
            local_d.start()
        else:
            group(d - 1, False)
    group(3, True)

    def all_picks():
        return (
            remote(pick.at[pl.ds(1, 7)], pick_in.at[pl.ds(1, 7)], os_.at[0], or_.at[0], partner),
            remote(weigh.at[pl.ds(1, 7)], weigh_in.at[pl.ds(1, 7)], os_.at[1], or_.at[1], partner),
        )

    for c in all_picks():
        c.wait_recv()
    loads[5].wait()
    choose[...] = jnp.dot(perm[...], pick_in[...].reshape(SLOTS, 128), preferred_element_type=F32).astype(BF)
    spread[...] = jnp.dot(perm[...], weigh_in[...].reshape(SLOTS, 128), preferred_element_type=F32).T.astype(BF)
    loads[6].wait()
    loads[7].wait()

    for d in (1, 2, 3):
        proj_copy(d).wait_recv()

    def att_copy(dy):
        return remote(att.at[0], att.at[dy], as_.at[dy - 1], ar.at[dy - 1], along_y(dy))

    for dy in (1, 2, 3):
        att_copy(dy).wait_recv()

    def core_part(j):
        return remote(part.at[j, 1 - core], other.at[j], d1s.at[j], d1r.at[j], partner)

    def x_copy(j, dx):
        i = j * 3 + dx - 1
        return remote(send_x.at[j, dx], from_x.at[j, dx - 1], d2s.at[i], d2r.at[i], along_x(dx))

    def yz_copy(j, dy, dz):
        i = j * 8 + dy * 2 + dz
        return remote(send_z.at[j, dy, dz], from_z.at[j, dy, dz], d3s.at[i], d3r.at[i], along_yz(dy, dz))

    def project(j):
        got = jnp.dot(att[...].reshape(1024, 512), proj[(z_lo + 4 - j) % 4], preferred_element_type=F32)
        got = got.astype(BF).reshape(4, 2, 4, 2, ROWS, 256)
        part[j, 0] = got[:, :, :, 0]
        part[j, 1] = got[:, :, :, 1]
        core_part(j).start()

    def sum_cores(j):
        core_part(j).wait_recv()
        for dx in (2, 1, 3, 0):
            xt = (x + dx) % 4
            for dz in range(2):
                zt = (z_hi + dz) % 2
                for dy in range(4):
                    mine = part[j, core, dy, zt, xt].astype(F32) + other[j, dy, zt, xt].astype(F32)
                    send_x[j, dx, dy, dz] = mine.astype(BF)
            if dx > 0:
                x_copy(j, dx).start()

    def sum_x(j):
        for dx in (1, 2, 3):
            x_copy(j, dx).wait_recv()
        for dz in (1, 0):
            for dy in (3, 2, 1, 0):
                got = send_x[j, 0, dy, dz].astype(F32) + from_x[j, 0, dy, dz].astype(F32)
                got = got + (from_x[j, 1, dy, dz].astype(F32) + from_x[j, 2, dy, dz].astype(F32))
                if dy + dz > 0:
                    send_z[j, dy, dz] = got.astype(BF)
                    yz_copy(j, dy, dz).start()
                else:
                    from_z[j, 0, 0] = got.astype(BF)

    def token_copy(c, d):
        return remote(tok.at[c, 0], tok.at[c, d], ts.at[c], tr.at[c], along_z(d))

    def all_tokens(c):
        return remote(tok.at[c, pl.ds(1, 7)], tok.at[c, pl.ds(1, 7)], ts.at[c], tr.at[c], partner)

    def sum_all(j, square):
        for dy in range(4):
            for dz in range(2):
                if dy + dz > 0:
                    yz_copy(j, dy, dz).wait_recv()
            ysrc = (y + dy) % 4
            cols = tile(j * 4 + ysrc)
            got = from_z[j, dy, 0].astype(F32) + from_z[j, dy, 1].astype(F32)
            state = (resid[:, cols].astype(F32) + got).astype(BF)
            hidden[:, cols] = state
            state = state.astype(F32)
            square = square + state * state
            per = CW // 256
            tok[j * SUB + ysrc // per, 0, :, tile(ysrc % per)] = (state * gain[:, cols]).astype(BF)
        for c in range(j * SUB, j * SUB + SUB):

            def one(d, _):
                token_copy(c, d).start()
                return 0

            lax.fori_loop(1, 8, one, 0)
        return square

    def all_rows(c):
        return remote(packed.at[c], rows.at[c, pl.ds(1, 15)], xs.at[c], xr.at[c], partner)

    def pack(j):
        def one(s, _):
            c = j * SUB + s
            all_tokens(c).wait_recv()

            def columns(n, _):
                got = jnp.dot(choose[...], tok[c, :, :, tile(n)].reshape(128, 256), preferred_element_type=F32)
                got = got.astype(BF).reshape(16, SLOT, 256)
                rows[c, 0, :, tile(n)] = got[0]
                packed[c, :, :, tile(n)] = got[1:]
                return 0

            lax.fori_loop(0, CW // 256, columns, 0)

            def send(i, _):
                remote(packed.at[c, i - 1], rows.at[c, i], xs.at[c], xr.at[c], in_plane(i)).start()
                return 0

            lax.fori_loop(1, 16, send, 0)
            return 0

        lax.fori_loop(0, SUB, one, 0)

    def scale_copy(d):
        return remote(scale.at[0], scale.at[d], ss.at[0], sr.at[0], along_z(d))

    def all_scales():
        return remote(scale.at[pl.ds(1, 7)], scale.at[pl.ds(1, 7)], ss.at[0], sr.at[0], partner)

    def all_slot_scales():
        return remote(scale_out, scale_in.at[pl.ds(1, 15)], ss.at[1], sr.at[1], partner)

    square = jnp.zeros((ROWS, 256), F32)
    for t in range(8):
        if t < 4:
            project(t)
        if 0 <= t - 1 < 4:
            sum_cores(t - 1)
        if 0 <= t - 2 < 4:
            sum_x(t - 2)
        if 0 <= t - 3 < 4:
            square = sum_all(t - 3, square)
        if t == 3:
            lax.fori_loop(0, NC, start_far, 0)
            far_d.start()
        if t == 6:
            mean = jnp.sum(square, axis=1, keepdims=True) * (1.0 / D)
            factor = jnp.broadcast_to(lax.rsqrt(mean + EPS), (ROWS, 128))
            coarse = factor.astype(BF)
            fine = (factor - coarse.astype(F32)).astype(BF)
            lane = lax.broadcasted_iota(jnp.int32, (ROWS, 128), 1)
            scale[0] = jnp.where(lane < 64, coarse.astype(F32), fine.astype(F32)).astype(BF)
            for d in range(1, 8):
                scale_copy(d).start()
        if 0 <= t - 4 < 4:
            pack(t - 4)

    all_scales().wait_recv()
    got = jnp.dot(choose[...], scale[...].reshape(128, 128), preferred_element_type=F32)
    got = got.astype(BF).reshape(16, SLOT, 128)
    scale_in[0] = got[0]
    scale_out[...] = got[1:]

    def send_scale(i, _):
        remote(scale_out.at[i - 1], scale_in.at[i], ss.at[1], sr.at[1], in_plane(i)).start()
        return 0

    lax.fori_loop(1, 16, send_scale, 0)

    acc_g[...] = jnp.zeros_like(acc_g)
    acc_u[...] = jnp.zeros_like(acc_u)

    def upward(c, _):
        local_g(c).wait()
        local_u(c).wait()
        far_g(c).wait_recv()
        far_u(c).wait_recv()
        all_rows(c).wait_recv()

        def columns(n, _):
            got = rows[c].reshape(SLOTS, CW)
            acc_g[:, tile(n)] += jnp.dot(got, wg[chunk(c), tile(n)], preferred_element_type=F32)
            acc_u[:, tile(n)] += jnp.dot(got, wu[chunk(c), tile(n)], preferred_element_type=F32)
            return 0

        lax.fori_loop(0, 3, columns, 0)
        return 0

    lax.fori_loop(0, NC, upward, 0)
    all_slot_scales().wait_recv()
    both = scale_in[...].reshape(SLOTS, 128).astype(F32)
    factor = both[:, 0:1] + both[:, 64:65]

    def activate(n, _):
        act[:, tile(n)] = (jax.nn.silu(acc_g[:, tile(n)] * factor) * (acc_u[:, tile(n)] * factor)).astype(BF)
        return 0

    lax.fori_loop(0, 3, activate, 0)
    local_d.wait()
    far_d.wait_recv()

    def all_back(c):
        return remote(back.at[c], ret.at[c, pl.ds(1, 15)], rs.at[c], rr.at[c], partner)

    def all_sums(c):
        return remote(summed.at[c, pl.ds(1, 7)], sums_in.at[c, pl.ds(1, 7)], fs.at[c], fr.at[c], partner)

    def downward(c, _):
        def columns(n, _):
            got = jnp.dot(act[...], wd[:, tile(c * (CW // 256) + n)], preferred_element_type=F32)
            got = got.astype(BF).reshape(16, SLOT, 256)
            ret[c, 0, :, tile(n)] = got[0]
            back[c, :, :, tile(n)] = got[1:]
            return 0

        lax.fori_loop(0, CW // 256, columns, 0)

        def send(i, _):
            remote(back.at[c, i - 1], ret.at[c, i], rs.at[c], rr.at[c], plane_back(i)).start()
            return 0

        lax.fori_loop(1, 16, send, 0)
        return 0

    lax.fori_loop(0, NC, downward, 0)

    def combine(c, _):
        all_back(c).wait_recv()

        def columns(n, _):
            got = ret[c, :, :, tile(n)].reshape(SLOTS, 256)
            got = jnp.dot(spread[...], got, preferred_element_type=F32)
            summed[c, :, :, tile(n)] = got.astype(BF).reshape(8, ROWS, 256)
            return 0

        lax.fori_loop(0, CW // 256, columns, 0)

        def send(d, _):
            remote(summed.at[c, d], sums_in.at[c, d], fs.at[c], fr.at[c], along_z(8 - d)).start()
            return 0

        lax.fori_loop(1, 8, send, 0)
        return 0

    lax.fori_loop(0, NC, combine, 0)

    def finish(c, _):
        all_sums(c).wait_recv()
        got = summed[c, 0].astype(F32)
        for d in range(1, 8):
            got = got + sums_in[c, d].astype(F32)
        out_ref[:, chunk(c)] = (hidden[:, chunk(c)].astype(F32) + got).astype(BF)
        return 0

    lax.fori_loop(0, NC, finish, 0)

    for d in (1, 2, 3):
        z_copy(d).wait_send()
        proj_copy(d).wait_send()
        att_copy(d).wait_send()
    for d in range(4):
        for dy in (1, 2, 3):
            y_copy(d, dy).wait_send()
        for dy in range(4):
            if d + dy > 0:
                core_copy(d, dy).wait_send()
    for j in range(4):
        core_part(j).wait_send()
        for dx in (1, 2, 3):
            x_copy(j, dx).wait_send()
        for dy in range(4):
            for dz in range(2):
                if dy + dz > 0:
                    yz_copy(j, dy, dz).wait_send()
    for c in all_picks():
        c.wait_send()
    all_scales().wait_send()
    all_slot_scales().wait_send()

    def drain(c, _):
        far_g(c).wait_send()
        far_u(c).wait_send()
        all_tokens(c).wait_send()
        all_rows(c).wait_send()
        all_back(c).wait_send()
        all_sums(c).wait_send()
        return 0

    lax.fori_loop(0, NC, drain, 0)
    far_d.wait_send()


def slot_order():
    perm = np.zeros((SLOTS, SLOTS), np.float32)
    for p in range(16):
        for s in range(8):
            for r in range(CAP):
                perm[p * SLOT + s * CAP + r, s * 16 * CAP + r * 16 + p] = 1.0
    return perm


VMEM = pl.BlockSpec(memory_space=pltpu.VMEM)
SMEM = pl.BlockSpec(memory_space=pltpu.SMEM)
ANY = pl.BlockSpec(memory_space=pl.ANY)
SHAPE = jax.ShapeDtypeStruct
DMA = pltpu.SemaphoreType.DMA


def both_ways(*counts):
    return [DMA((n,)) for n in counts for _ in range(2)]


def layer(*operands):
    return pl.pallas_call(
        layer_kernel,
        out_shape=SHAPE((ROWS, D), BF),
        in_specs=[SMEM] + [ANY] * 11,
        out_specs=VMEM,
        scratch_shapes=[
            pltpu.VMEM((256, 512), BF),
            pltpu.VMEM((ROWS, D), BF),
            pltpu.VMEM((1, D), F32),
            pltpu.VMEM((2 * TOP, 128), F32),
            pltpu.VMEM((SLOTS, SLOTS), BF),
            pltpu.VMEM((2, 4, 4, 272, HEAD), BF),
            pltpu.VMEM((4, 256, 256), F32),
            pltpu.VMEM((256, HEAD), F32),
            pltpu.VMEM((4, 256, HEAD), F32),
            pltpu.VMEM((4, 256, HEAD), F32),
            pltpu.VMEM((4, 256, HEAD), F32),
            pltpu.VMEM((4, 256, 512), BF),
            pltpu.VMEM((4, 512, 256), BF),
            pltpu.VMEM((4, 2, 4, 2, 4, ROWS, 256), BF),
            pltpu.VMEM((4, 4, 2, 4, ROWS, 256), BF),
            pltpu.VMEM((4, 4, 4, 2, ROWS, 256), BF),
            pltpu.VMEM((4, 3, 4, 2, ROWS, 256), BF),
            pltpu.VMEM((4, 4, 2, ROWS, 256), BF),
            pltpu.VMEM((4, 4, 2, ROWS, 256), BF),
            pltpu.VMEM((ROWS, D), BF),
            pltpu.VMEM((D, 2 * FH), BF),
            pltpu.VMEM((D, 2 * FH), BF),
            pltpu.VMEM((2 * FH, D), BF),
            pltpu.VMEM((8, CAP, 16, 128), BF),
            pltpu.VMEM((8, CAP, 16, 128), BF),
            pltpu.VMEM((8, CAP, 16, 128), BF),
            pltpu.VMEM((8, CAP, 16, 128), BF),
            pltpu.VMEM((SLOTS, 128), BF),
            pltpu.VMEM((128, SLOTS), BF),
            pltpu.VMEM((NC, 8, ROWS, CW), BF),
            pltpu.VMEM((8, ROWS, 128), BF),
            pltpu.VMEM((NC, 15, SLOT, CW), BF),
            pltpu.VMEM((NC, 16, SLOT, CW), BF),
            pltpu.VMEM((15, SLOT, 128), BF),
            pltpu.VMEM((16, SLOT, 128), BF),
            pltpu.VMEM((SLOTS, 2 * FH), F32),
            pltpu.VMEM((SLOTS, 2 * FH), F32),
            pltpu.VMEM((SLOTS, 2 * FH), BF),
            pltpu.VMEM((NC, 15, SLOT, CW), BF),
            pltpu.VMEM((NC, 16, SLOT, CW), BF),
            pltpu.VMEM((NC, 8, ROWS, CW), BF),
            pltpu.VMEM((NC, 8, ROWS, CW), BF),
            DMA((8,)),
            *both_ways(3, 12, 16, 3, 3, 4, 12, 32),
            DMA((NC,)), DMA((NC,)), DMA((1,)),
            *both_ways(NC, NC, 1, 2, NC, 2, NC, NC, NC),
        ],
        compiler_params=pltpu.CompilerParams(
            collective_id=0, has_side_effects=True, vmem_limit_bytes=60 * 1024 * 1024
        ),
        name="layer",
    )(*operands)


def local(
    queries,
    key_states,
    value_head_states,
    block_order,
    out_proj,
    residual,
    norm_gain,
    w_gate,
    w_up,
    w_down,
    routes,
    gate_weights,
):
    routing = jnp.concatenate([routes.astype(F32), gate_weights], axis=1)
    routing = jnp.tile(routing.T, (1, 8))
    perm = jnp.asarray(slot_order(), BF)
    return layer(
        block_order, queries, key_states, value_head_states, out_proj, residual,
        norm_gain.reshape(1, D), routing, perm, w_gate, w_up, w_down,
    )


def solution(mesh):
    return jax.shard_map(
        local,
        mesh=mesh,
        in_specs=(
            P("ctx", "ep"),
            P("ctx", None),
            P("ctx", None),
            P("ctx"),
            P("ep", "ctx"),
            P(("ctx", "ep"), None),
            P(),
            P(None, ("ctx", "ep")),
            P(None, ("ctx", "ep")),
            P(("ctx", "ep"), None),
            P(("ctx", "ep"), None),
            P(("ctx", "ep"), None),
        ),
        out_specs=P(("ctx", "ep"), None),
        check_vma=False,
    )
```

time: 1220 us -> 159 us (0.13)
  the two profiles are of different devices: /device:TPU:151 before, /device:TPU:2 now
where the time goes in v2:
time: 159 us
  Pallas kernels  156 us (98%)
  local copies, waits for them, and re-layouts  2.26 us (1%)
    pallas_call x1, Pallas kernels, layer(): pl.pallas_call(layer_kernel, out_shape=SHAPE((ROWS, D), BF), in_specs=[SM...  156 us

profile of v2, /device:TPU:2, one launch (start us, length us, event | category | flops | bytes accessed | tf_op | source)
XLA Modules:
  0.0 159.3 jit_solution(972064049030257802)
XLA Ops:
  0.0 0.7 convert_element_type.3
  0.7 0.7 maximum_bitcast_fusion
  1.4 0.7 tile.10.routes_hbm
  2.1 155.7 %layer.1 = bf16[16,4096]{1,0:T(8,128)(2,1)} custom-call(s32[2]{0:T(128)} %order_ref.1, bf16[256,512]{1,0:T(8,128)(2,1)} %q_hbm.1, bf16[256,512]{1,0:T(8,128)(2,1)} %k_hbm.1, bf16[256,512]{1,0:T(8,128)(2,1)} %v_hbm.1, bf16[512,256]{1,0:T(8,128)(2,1)} %proj_hbm.1, bf16[16,4096]{1,0:T(8,128)(2,1)} %resid_hbm.1, f32[1,4096]{1,0:T(1,128)} %bitcast.3, ...), custom_call_target="tpu_custom_call" | custom-call | tf_op jit(solution)/shard_map/layer/pallas_call | solution.py:602
  157.7 1.6 copy.15
  (1 shorter events, 0.0 us)

commit v3 on v2

v3 whole, which is shorter than its diff:
```python
import math

import jax
import jax.numpy as jnp
import numpy as np
from jax import lax
from jax.experimental import pallas as pl
from jax.experimental.pallas import tpu as pltpu
from jax.sharding import PartitionSpec as P

MESH = pl.DeviceIdType.MESH
BF = jnp.bfloat16
F32 = jnp.float32

D = 4096
HEAD = 128
TOP = 8
NEG = -1e30
EPS = 1e-06
SCALE2 = math.log2(math.e) / math.sqrt(HEAD)

SUB = 2
NC = 4 * SUB
CW = D // NC
ROWS = 16
CAP = 3
SLOT = 8 * CAP
SLOTS = 16 * SLOT
FH = 384


def here():
    c = lax.axis_index("ctx")
    e = lax.axis_index("ep")
    return (e // 2) % 4, c % 4, e // 8, c // 4, e % 2


def device(x, y, z_hi, z_lo, core):
    return (z_lo * 4 + y, z_hi * 8 + x * 2 + core)


def remote(src, dst, send, recv, target):
    return pltpu.make_async_remote_copy(
        src_ref=src, dst_ref=dst, send_sem=send, recv_sem=recv, device_id=target, device_id_type=MESH
    )


def layer_kernel(
    order_ref, q_hbm, k_hbm, v_hbm, proj_hbm, resid_hbm, gain_hbm, routes_hbm, gates_hbm, perm_hbm, wg_hbm, wu_hbm, wd_hbm,
    out_ref,
    query, resid, gain, routes, gates, perm,
    kv, scores, qpos, peak, total, acc, att, proj, part, other, send_x, from_x, send_z, from_z, hidden,
    wg, wu, wd, weigh, weigh_in, choose, spread,
    tok, scale, packed, rows, scale_out, scale_in, acc_g, acc_u, act, back, ret, summed, sums_in,
    load_sem, zs, zr, ys, yr, cs, cr, rights, rightr, lefts, leftr, as_, ar, d1s, d1r, d2s, d2r, d3s, d3r,
    lg, lu, ld, gs, gr, us, ur, ws, wr, os_, or_, ts, tr, ss, sr, xs, xr, rs, rr, fs, fr,
):
    x, y, z_hi, z_lo, core = here()
    z = z_hi * 4 + z_lo
    partner = device(x, y, z_hi, z_lo, 1 - core)

    def in_span(d):
        return device(x, y, z_hi, (z_lo + d) % 4, core)

    def along_y(d):
        return device(x, (y + d) % 4, z_hi, z_lo, core)

    def along_x(d):
        return device((x + d) % 4, y, z_hi, z_lo, core)

    def along_yz(dy, dz):
        return device(x, (y + 4 - dy) % 4, (z_hi + dz) % 2, z_lo, core)

    def along_z(d):
        to = (z + d) % 8
        return device(x, y, to // 4, to % 4, core)

    def in_plane(i):
        return device((x + i % 4) % 4, (y + i // 4) % 4, z_hi, z_lo, core)

    def plane_back(i):
        return device((x + 4 - i % 4) % 4, (y + 4 - i // 4) % 4, z_hi, z_lo, core)

    def chunk(c):
        return pl.ds(pl.multiple_of(c * CW, CW), CW)

    def tile(n):
        return pl.ds(pl.multiple_of(n * 256, 256), 256)

    head_col = pl.multiple_of((z_hi * 2 + x // 2) * HEAD, HEAD)
    loads = [
        pltpu.make_async_copy(src, dst, load_sem.at[i])
        for i, (src, dst) in enumerate([
            (k_hbm.at[:, pl.ds(head_col, HEAD)], kv.at[0, 0, 0, pl.ds(0, 256), :]),
            (v_hbm.at[:, pl.ds(head_col, HEAD)], kv.at[1, 0, 0, pl.ds(0, 256), :]),
            (proj_hbm, proj.at[z_lo]),
            (q_hbm, query),
            (routes_hbm, routes),
            (perm_hbm, perm),
            (resid_hbm, resid),
            (gain_hbm, gain),
            (gates_hbm, gates),
        ])
    ]
    for c in loads:
        c.start()

    barrier = pltpu.get_barrier_semaphore()

    def greet(target):
        pl.semaphore_signal(barrier, inc=1, device_id=target, device_id_type=MESH)

    def greet_z(d, _):
        greet(along_z(d))
        return 0

    def greet_plane(i, _):
        greet(in_plane(i))
        return 0

    greet(partner)
    lax.fori_loop(1, 8, greet_z, 0)
    lax.fori_loop(1, 16, greet_plane, 0)
    for dy in (1, 2, 3):
        greet(along_yz(dy, 1))

    first = order_ref[0].astype(F32)
    second = order_ref[1].astype(F32)
    row16 = lax.broadcasted_iota(jnp.int32, (16, HEAD), 0)
    tail = jnp.where(row16 < 8, first, second).astype(BF)
    kv[0, 0, 0, 256:272, :] = tail
    kv[1, 0, 0, 256:272, :] = tail
    row = lax.broadcasted_iota(jnp.int32, (256, HEAD), 0)
    qpos[...] = jnp.where(row < 128, first * 128.0 + row.astype(F32), (second - 1.0) * 128.0 + row.astype(F32))

    loads[0].wait()
    loads[1].wait()
    pl.semaphore_wait(barrier, 26)

    def z_copy(d):
        return remote(kv.at[core, 0, 0], kv.at[core, d, 0], zs.at[d - 1], zr.at[d - 1], in_span(d))

    def y_copy(d, dy):
        i = d * 3 + dy - 1
        return remote(kv.at[core, d, 0], kv.at[core, d, dy], ys.at[i], yr.at[i], along_y(dy))

    def core_copy(d, dy):
        i = d * 4 + dy
        return remote(kv.at[core, d, dy], kv.at[core, d, dy], cs.at[i], cr.at[i], partner)

    def core_arrival(d, dy):
        i = d * 4 + dy
        return remote(kv.at[1 - core, d, dy], kv.at[1 - core, d, dy], cs.at[i], cr.at[i], partner)

    def right_copy(p, slot):
        return remote(proj.at[slot], proj.at[slot], rights.at[p], rightr.at[p], in_span(1))

    def left_copy(p, slot):
        return remote(proj.at[slot], proj.at[slot], lefts.at[p], leftr.at[p], in_span(3))

    def proj_send(p):
        @pl.when((z_lo <= 2) & (z_lo >= p))
        def _():
            right_copy(p, z_lo - p).start()

        @pl.when((z_lo >= 1) & (z_lo + p <= 3))
        def _():
            left_copy(p, z_lo + p).start()

    def proj_arrival(p):
        @pl.when(z_lo >= p + 1)
        def _():
            right_copy(p, z_lo - 1 - p).wait_recv()

        @pl.when(z_lo <= 2 - p)
        def _():
            left_copy(p, z_lo + 1 + p).wait_recv()

    def proj_sent(p):
        @pl.when((z_lo <= 2) & (z_lo >= p))
        def _():
            right_copy(p, z_lo - p).wait_send()

        @pl.when((z_lo >= 1) & (z_lo + p <= 3))
        def _():
            left_copy(p, z_lo + p).wait_send()

    for d in (1, 2, 3):
        z_copy(d).start()
    for dy in (1, 2, 3):
        y_copy(0, dy).start()

    loads[4].wait()
    loads[8].wait()
    token = lax.broadcasted_iota(jnp.int32, (ROWS, 128), 0)
    lane = lax.broadcasted_iota(jnp.int32, (ROWS, 128), 1)
    repeat = jnp.where((lane & 15) == token, 1.0, 0.0)
    named_by = jnp.dot(routes[...].astype(F32), repeat, preferred_element_type=F32)
    weight_by = jnp.dot(gates[...], repeat, preferred_element_type=F32)
    row = lax.broadcasted_iota(jnp.int32, (128, 128), 0)
    lane = lax.broadcasted_iota(jnp.int32, (128, 128), 1)
    z_to = (z + (row >> 4)) & 7
    x_to = (x + (row & 3)) & 3
    y_to = (y + ((row >> 2) & 3)) & 3
    expert = ((z_to & 3) * 32 + y_to * 8 + (z_to >> 2) * 4 + x_to).astype(F32)
    own = (lane >> 4) == (row >> 4)
    named = jnp.zeros((128, 128), F32)
    weight = jnp.zeros((128, 128), F32)
    for j in range(TOP):
        hit = jnp.where(own & (jnp.abs(named_by[j : j + 1, :] - expert) < 0.5), 1.0, 0.0)
        named = named + hit
        weight = weight + hit * weight_by[j : j + 1, :]
    before = jnp.where(row < lane, 1.0, 0.0).astype(BF)
    rank = jnp.dot(named.astype(BF), before, preferred_element_type=F32)
    for r in range(CAP):
        at = jnp.where((named > 0.5) & (jnp.abs(rank - r) < 0.5), 1.0, 0.0)
        weigh[:, r] = (at * weight).reshape(8, 16, 128).astype(BF)

    for d in (1, 2, 3):
        z_copy(d).wait_recv()
        if d == 1:
            loads[2].wait()
            proj_send(0)
        for dy in (1, 2, 3):
            y_copy(d, dy).start()
        core_copy(d, 0).start()
    def weigh_copy(d):
        return remote(weigh.at[d], weigh_in.at[d], os_.at[0], or_.at[0], along_z(d))

    def all_weigh():
        return remote(weigh.at[pl.ds(1, 7)], weigh_in.at[pl.ds(1, 7)], os_.at[0], or_.at[0], partner)

    def send_weigh(d, _):
        weigh_copy(d).start()
        return 0

    weigh_in[0] = weigh[0]

    own_half = pl.ds(0, FH)
    far_half = pl.ds(FH, FH)

    def from_rows(f, b):
        return pl.ds(pl.multiple_of((b * 4 + f) * 256, 256), 256)

    def local_weights(f):
        for b in range(4):
            pltpu.make_async_copy(wg_hbm.at[from_rows(f, b), :], wg.at[f, pl.ds(b * 256, 256), own_half], lg.at[f]).start()
            pltpu.make_async_copy(wu_hbm.at[from_rows(f, b), :], wu.at[f, pl.ds(b * 256, 256), own_half], lu.at[f]).start()

    def far_weights(f):
        for b in range(4):
            remote(wg_hbm.at[from_rows(f, b), :], wg.at[f, pl.ds(b * 256, 256), far_half], gs.at[f], gr.at[f], partner).start()
            remote(wu_hbm.at[from_rows(f, b), :], wu.at[f, pl.ds(b * 256, 256), far_half], us.at[f], ur.at[f], partner).start()

    def all_local(f):
        return (
            pltpu.make_async_copy(wg_hbm.at[pl.ds(0, 1024), :], wg.at[f, :, own_half], lg.at[f]),
            pltpu.make_async_copy(wu_hbm.at[pl.ds(0, 1024), :], wu.at[f, :, own_half], lu.at[f]),
        )

    def all_far(f):
        return (
            remote(wg_hbm.at[pl.ds(0, 1024), :], wg.at[f, :, far_half], gs.at[f], gr.at[f], partner),
            remote(wu_hbm.at[pl.ds(0, 1024), :], wu.at[f, :, far_half], us.at[f], ur.at[f], partner),
        )

    local_d = pltpu.make_async_copy(wd_hbm, wd.at[own_half, :], ld.at[0])
    far_d = remote(wd_hbm, wd.at[far_half, :], ws.at[0], wr.at[0], partner)

    def start_local(f, _):
        local_weights(f)
        return 0

    def start_far(f, _):
        far_weights(f)
        return 0

    lanes = lax.broadcasted_iota(jnp.int32, (8, HEAD), 1).astype(F32)
    loads[3].wait()

    def group(d, last):
        for dy in range(4):
            if d + dy > 0:
                core_arrival(d, dy).wait_recv()

        def score(h, side):
            q = query[:, pl.ds(pl.multiple_of(h * HEAD, HEAD), HEAD)]
            top = None
            for dy in range(4):
                ids = kv[0, d, dy, 256:272, :].astype(F32) * 128.0
                got = lax.dot_general(
                    q, kv[0, d, dy, 0:256, :], (((1,), (1,)), ((), ())), preferred_element_type=F32
                )
                left = jnp.where((ids[0:8] + lanes)[0:1] <= qpos[...], got[:, :HEAD], NEG)
                right = jnp.where((ids[8:16] + lanes)[0:1] <= qpos[...], got[:, HEAD:], NEG)
                scores[side, dy, :, 0:HEAD] = left
                scores[side, dy, :, HEAD:256] = right
                both = jnp.maximum(left, right)
                top = both if top is None else jnp.maximum(top, both)
            return jnp.broadcast_to(jnp.max(top, axis=1, keepdims=True), (256, HEAD))

        def gather(h, side, now):
            cols = pl.ds(pl.multiple_of(h * HEAD, HEAD), HEAD)
            if d > 0:
                old = peak[h]
                now = jnp.maximum(now, old)
                shrink = jnp.exp2((old - now) * SCALE2)
                sums = total[h] * shrink
                out = acc[h] * shrink
            else:
                sums = jnp.zeros((256, HEAD), F32)
                out = jnp.zeros((256, HEAD), F32)
            peak[h] = now
            for dy in range(4):
                left = jnp.exp2((scores[side, dy, :, 0:HEAD] - now) * SCALE2)
                right = jnp.exp2((scores[side, dy, :, HEAD:256] - now) * SCALE2)
                both = jnp.concatenate([left.astype(BF), right.astype(BF)], axis=1)
                out = out + jnp.dot(both, kv[1, d, dy, 0:256, :], preferred_element_type=F32)
                sums = sums + (left + right)
            if last:
                att[0, :, cols] = (out / jnp.sum(sums, axis=1, keepdims=True)).astype(BF)
                for dy in (1, 3, 2):
                    remote(att.at[0, :, cols], att.at[dy, :, cols], as_.at[dy - 1], ar.at[dy - 1], along_y(dy)).start()
            else:
                total[h] = sums
                acc[h] = out

        def two_heads(i, _):
            even = score(2 * i, 0)
            odd = score(2 * i + 1, 1)
            gather(2 * i, 0, even)
            gather(2 * i + 1, 1, odd)
            return 0

        lax.fori_loop(0, 2, two_heads, 0)

    for d in range(4):
        for dy in (1, 2, 3):
            y_copy(d, dy).wait_recv()
            core_copy(d, dy).start()
        if d == 0:
            lax.fori_loop(0, 4, start_local, 0)
            local_d.start()
        else:
            if d == 1 or d == 3:
                proj_arrival(d // 2)
                proj_send(d // 2 + 1)
            group(d - 1, False)
    group(3, True)
    lax.fori_loop(1, 8, send_weigh, 0)

    def att_copy(dy):
        return remote(att.at[0], att.at[dy], as_.at[dy - 1], ar.at[dy - 1], along_y(dy))

    def core_part(dy):
        return remote(part.at[dy, 1 - core], other.at[dy], d1s.at[dy], d1r.at[dy], partner)

    def x_copy(dy, dx):
        i = dy * 3 + dx - 1
        return remote(send_x.at[dy, dx], from_x.at[dy, dx - 1], d2s.at[i], d2r.at[i], along_x(dx))

    def yz_copy(dy, dz):
        i = dy * 2 + dz
        return remote(send_z.at[dy, dz], from_z.at[dy, dz], d3s.at[i], d3r.at[i], along_yz(dy, dz))

    def project(dy):
        if dy > 0:
            att_copy(dy).wait_recv()
        for b in range(4):
            got = jnp.dot(att[dy], proj[b], preferred_element_type=F32)
            got = got.astype(BF).reshape(2, 4, 2, ROWS, 256)
            part[dy, 0, :, :, :, b * 256 : b * 256 + 256] = got[:, :, 0]
            part[dy, 1, :, :, :, b * 256 : b * 256 + 256] = got[:, :, 1]
        core_part(dy).start()

    def sum_cores(dy):
        core_part(dy).wait_recv()
        for dx in (2, 1, 3, 0):
            xt = (x + dx) % 4
            for dz in range(2):
                zt = (z_hi + dz) % 2
                mine = part[dy, core, zt, xt].astype(F32) + other[dy, zt, xt].astype(F32)
                send_x[dy, dx, dz] = mine.astype(BF)
            if dx > 0:
                x_copy(dy, dx).start()

    def sum_x(dy):
        for dx in (1, 2, 3):
            x_copy(dy, dx).wait_recv()
        for dz in (1, 0):
            got = send_x[dy, 0, dz].astype(F32) + from_x[dy, 0, dz].astype(F32)
            got = got + (from_x[dy, 1, dz].astype(F32) + from_x[dy, 2, dz].astype(F32))
            if dy + dz > 0:
                send_z[dy, dz] = got.astype(BF)
                yz_copy(dy, dz).start()
            else:
                from_z[0, 0] = got.astype(BF)

    def token_copy(dy, slot, step):
        to = (slot + step) % 8
        return remote(
            tok.at[dy, slot], tok.at[dy, to], ts.at[dy * 8 + to], tr.at[dy * 8 + to], along_z(1 if step == 1 else 7)
        )

    def last_step(dy):
        return (3, 1) if dy % 2 == 0 else (5, 7)

    def token_moves(dy):
        return [[(0, 1), (0, 7)], [(1, 1), (7, 7)], [(2, 1), (6, 7)], [last_step(dy)]]

    def forward(dy, hop):
        for slot, step in token_moves(dy)[hop - 1]:
            if hop > 1:
                token_copy(dy, (slot - step) % 8, step).wait_recv()
            token_copy(dy, slot, step).start()

    def sum_all(dy, square):
        for dz in range(2):
            if dy + dz > 0:
                yz_copy(dy, dz).wait_recv()
        from_y = (y + dy) % 4
        for b in range(4):
            cols = tile(b * 4 + from_y)
            near = slice(b * 256, b * 256 + 256)
            got = from_z[dy, 0, :, near].astype(F32) + from_z[dy, 1, :, near].astype(F32)
            state = (resid[:, cols].astype(F32) + got).astype(BF)
            hidden[:, cols] = state
            state = state.astype(F32)
            square = square + state * state
            tok[dy, 0, :, near] = (state * gain[:, cols]).astype(BF)
        forward(dy, 1)
        return square

    def all_rows(c):
        return remote(packed.at[c], rows.at[c, pl.ds(1, 15)], xs.at[c], xr.at[c], partner)

    def pack(dy):
        slot, step = last_step(dy)
        token_copy(dy, slot, step).wait_recv()
        slot, step = token_moves(dy)[2][1 if dy % 2 == 0 else 0]
        token_copy(dy, slot, step).wait_recv()

        def one(s, _):
            c = dy * SUB + s

            def columns(n, _):
                got = tok[dy, :, :, tile(s * (CW // 256) + n)].reshape(128, 256)
                got = jnp.dot(choose[...], got, preferred_element_type=F32)
                got = got.astype(BF).reshape(16, SLOT, 256)
                rows[c, 0, :, tile(n)] = got[0]
                packed[c, :, :, tile(n)] = got[1:]
                return 0

            lax.fori_loop(0, CW // 256, columns, 0)

            def send(i, _):
                remote(packed.at[c, i - 1], rows.at[c, i], xs.at[c], xr.at[c], in_plane(i)).start()
                return 0

            lax.fori_loop(1, 16, send, 0)
            return 0

        lax.fori_loop(0, SUB, one, 0)

    def scale_copy(d):
        return remote(scale.at[0], scale.at[d], ss.at[0], sr.at[0], along_z(d))

    def all_scales():
        return remote(scale.at[pl.ds(1, 7)], scale.at[pl.ds(1, 7)], ss.at[0], sr.at[0], partner)

    def all_slot_scales():
        return remote(scale_out, scale_in.at[pl.ds(1, 15)], ss.at[1], sr.at[1], partner)

    loads[5].wait()
    loads[6].wait()
    loads[7].wait()
    proj_arrival(2)
    square = jnp.zeros((ROWS, 256), F32)
    project(0)

    all_weigh().wait_recv()
    slots = jnp.dot(perm[...], weigh_in[...].reshape(SLOTS, 128), preferred_element_type=F32)
    choose[...] = jnp.where(slots > 0.0, 1.0, 0.0).astype(BF)
    spread[...] = slots.T.astype(BF)

    sum_cores(0)
    project(1)
    sum_x(0)
    sum_cores(1)
    project(3)
    sum_x(1)
    sum_cores(3)
    square = sum_all(0, square)
    project(2)
    forward(0, 2)
    sum_x(3)
    sum_cores(2)
    square = sum_all(1, square)
    forward(0, 3)
    forward(1, 2)
    forward(0, 4)
    sum_x(2)
    square = sum_all(3, square)
    forward(1, 3)
    forward(3, 2)
    pack(0)
    lax.fori_loop(0, 4, start_far, 0)
    far_d.start()
    forward(1, 4)
    square = sum_all(2, square)
    forward(3, 3)
    forward(2, 2)
    pack(1)
    forward(3, 4)
    forward(2, 3)
    mean = jnp.sum(square, axis=1, keepdims=True) * (1.0 / D)
    factor = jnp.broadcast_to(lax.rsqrt(mean + EPS), (ROWS, 128))
    coarse = factor.astype(BF)
    fine = (factor - coarse.astype(F32)).astype(BF)
    lane = lax.broadcasted_iota(jnp.int32, (ROWS, 128), 1)
    scale[0] = jnp.where(lane < 64, coarse.astype(F32), fine.astype(F32)).astype(BF)
    for d in range(1, 8):
        scale_copy(d).start()
    pack(3)
    forward(2, 4)
    pack(2)

    all_scales().wait_recv()
    got = jnp.dot(choose[...], scale[...].reshape(128, 128), preferred_element_type=F32)
    got = got.astype(BF).reshape(16, SLOT, 128)
    scale_in[0] = got[0]
    scale_out[...] = got[1:]

    def send_scale(i, _):
        remote(scale_out.at[i - 1], scale_in.at[i], ss.at[1], sr.at[1], in_plane(i)).start()
        return 0

    lax.fori_loop(1, 16, send_scale, 0)

    acc_g[...] = jnp.zeros_like(acc_g)
    acc_u[...] = jnp.zeros_like(acc_u)

    def weights_here(f, _):
        for c in all_local(f):
            c.wait()
        for c in all_far(f):
            c.wait_recv()
        return 0

    lax.fori_loop(0, 4, weights_here, 0)

    def upward(s, dy):
        c = dy * SUB + s
        all_rows(c).wait_recv()

        def one(q, _):
            f = (y + 4 - q + dy) % 4
            got = rows[c, pl.ds(q * 4, 4)].reshape(4 * SLOT, CW)
            at = pl.ds(pl.multiple_of(q * 4 * SLOT, 4 * SLOT), 4 * SLOT)
            depth = pl.ds(pl.multiple_of(s * CW, CW), CW)
            for n in range(3):
                cols = slice(n * 256, n * 256 + 256)
                acc_g[at, cols] += jnp.dot(got, wg[f, depth, cols], preferred_element_type=F32)
                acc_u[at, cols] += jnp.dot(got, wu[f, depth, cols], preferred_element_type=F32)
            return 0

        lax.fori_loop(0, 4, one, 0)
        return dy

    for dy in (0, 1, 3, 2):
        lax.fori_loop(0, SUB, upward, dy)
    all_slot_scales().wait_recv()
    both = scale_in[...].reshape(SLOTS, 128).astype(F32)
    factor = both[:, 0:1] + both[:, 64:65]

    def activate(n, _):
        act[:, tile(n)] = (jax.nn.silu(acc_g[:, tile(n)] * factor) * (acc_u[:, tile(n)] * factor)).astype(BF)
        return 0

    lax.fori_loop(0, 3, activate, 0)
    local_d.wait()
    far_d.wait_recv()

    def all_back(c):
        return remote(back.at[c], ret.at[c, pl.ds(1, 15)], rs.at[c], rr.at[c], partner)

    def all_sums(c):
        return remote(summed.at[c, pl.ds(1, 7)], sums_in.at[c, pl.ds(1, 7)], fs.at[c], fr.at[c], partner)

    def downward(c, _):
        def columns(n, _):
            got = jnp.dot(act[...], wd[:, tile(c * (CW // 256) + n)], preferred_element_type=F32)
            got = got.astype(BF).reshape(16, SLOT, 256)
            ret[c, 0, :, tile(n)] = got[0]
            back[c, :, :, tile(n)] = got[1:]
            return 0

        lax.fori_loop(0, CW // 256, columns, 0)

        def send(i, _):
            remote(back.at[c, i - 1], ret.at[c, i], rs.at[c], rr.at[c], plane_back(i)).start()
            return 0

        lax.fori_loop(1, 16, send, 0)
        return 0

    lax.fori_loop(0, NC, downward, 0)

    def combine(c, _):
        all_back(c).wait_recv()

        def columns(n, _):
            got = ret[c, :, :, tile(n)].reshape(SLOTS, 256)
            got = jnp.dot(spread[...], got, preferred_element_type=F32)
            summed[c, :, :, tile(n)] = got.astype(BF).reshape(8, ROWS, 256)
            return 0

        lax.fori_loop(0, CW // 256, columns, 0)

        def send(d, _):
            remote(summed.at[c, d], sums_in.at[c, d], fs.at[c], fr.at[c], along_z(8 - d)).start()
            return 0

        lax.fori_loop(1, 8, send, 0)
        return 0

    lax.fori_loop(0, NC, combine, 0)

    def finish(c, _):
        all_sums(c).wait_recv()
        got = summed[c, 0].astype(F32)
        for d in range(1, 8):
            got = got + sums_in[c, d].astype(F32)
        out_ref[:, chunk(c)] = (hidden[:, chunk(c)].astype(F32) + got).astype(BF)
        return 0

    lax.fori_loop(0, NC, finish, 0)

    for d in (1, 2, 3):
        z_copy(d).wait_send()
        proj_sent(d - 1)
        att_copy(d).wait_send()
    for d in range(4):
        for dy in (1, 2, 3):
            y_copy(d, dy).wait_send()
        for dy in range(4):
            if d + dy > 0:
                core_copy(d, dy).wait_send()
    for dy in range(4):
        core_part(dy).wait_send()
        for dx in (1, 2, 3):
            x_copy(dy, dx).wait_send()
        for dz in range(2):
            if dy + dz > 0:
                yz_copy(dy, dz).wait_send()
        for moves in token_moves(dy):
            for slot, step in moves:
                token_copy(dy, slot, step).wait_send()
        for c in all_far(dy):
            c.wait_send()
    all_weigh().wait_send()
    all_scales().wait_send()
    all_slot_scales().wait_send()

    def drain(c, _):
        all_rows(c).wait_send()
        all_back(c).wait_send()
        all_sums(c).wait_send()
        return 0

    lax.fori_loop(0, NC, drain, 0)
    far_d.wait_send()


def slot_order():
    perm = np.zeros((SLOTS, SLOTS), np.float32)
    for p in range(16):
        for s in range(8):
            for r in range(CAP):
                perm[p * SLOT + s * CAP + r, s * 16 * CAP + r * 16 + p] = 1.0
    return perm


VMEM = pl.BlockSpec(memory_space=pltpu.VMEM)
SMEM = pl.BlockSpec(memory_space=pltpu.SMEM)
ANY = pl.BlockSpec(memory_space=pl.ANY)
SHAPE = jax.ShapeDtypeStruct
DMA = pltpu.SemaphoreType.DMA


def both_ways(*counts):
    return [DMA((n,)) for n in counts for _ in range(2)]


def layer(*operands):
    return pl.pallas_call(
        layer_kernel,
        out_shape=SHAPE((ROWS, D), BF),
        in_specs=[SMEM] + [ANY] * 12,
        out_specs=VMEM,
        scratch_shapes=[
            pltpu.VMEM((256, 512), BF),
            pltpu.VMEM((ROWS, D), BF),
            pltpu.VMEM((1, D), F32),
            pltpu.VMEM((TOP, ROWS), jnp.int32),
            pltpu.VMEM((TOP, ROWS), F32),
            pltpu.VMEM((SLOTS, SLOTS), BF),
            pltpu.VMEM((2, 4, 4, 272, HEAD), BF),
            pltpu.VMEM((2, 4, 256, 256), F32),
            pltpu.VMEM((256, HEAD), F32),
            pltpu.VMEM((4, 256, HEAD), F32),
            pltpu.VMEM((4, 256, HEAD), F32),
            pltpu.VMEM((4, 256, HEAD), F32),
            pltpu.VMEM((4, 256, 512), BF),
            pltpu.VMEM((4, 512, 256), BF),
            pltpu.VMEM((4, 2, 2, 4, ROWS, 1024), BF),
            pltpu.VMEM((4, 2, 4, ROWS, 1024), BF),
            pltpu.VMEM((4, 4, 2, ROWS, 1024), BF),
            pltpu.VMEM((4, 3, 2, ROWS, 1024), BF),
            pltpu.VMEM((4, 2, ROWS, 1024), BF),
            pltpu.VMEM((4, 2, ROWS, 1024), BF),
            pltpu.VMEM((ROWS, D), BF),
            pltpu.VMEM((4, 1024, 2 * FH), BF),
            pltpu.VMEM((4, 1024, 2 * FH), BF),
            pltpu.VMEM((2 * FH, D), BF),
            pltpu.VMEM((8, CAP, 16, 128), BF),
            pltpu.VMEM((8, CAP, 16, 128), BF),
            pltpu.VMEM((SLOTS, 128), BF),
            pltpu.VMEM((128, SLOTS), BF),
            pltpu.VMEM((4, 8, ROWS, 1024), BF),
            pltpu.VMEM((8, ROWS, 128), BF),
            pltpu.VMEM((NC, 15, SLOT, CW), BF),
            pltpu.VMEM((NC, 16, SLOT, CW), BF),
            pltpu.VMEM((15, SLOT, 128), BF),
            pltpu.VMEM((16, SLOT, 128), BF),
            pltpu.VMEM((SLOTS, 2 * FH), F32),
            pltpu.VMEM((SLOTS, 2 * FH), F32),
            pltpu.VMEM((SLOTS, 2 * FH), BF),
            pltpu.VMEM((NC, 15, SLOT, CW), BF),
            pltpu.VMEM((NC, 16, SLOT, CW), BF),
            pltpu.VMEM((NC, 8, ROWS, CW), BF),
            pltpu.VMEM((NC, 8, ROWS, CW), BF),
            DMA((9,)),
            *both_ways(3, 12, 16, 3, 3, 3, 4, 12, 8),
            DMA((4,)), DMA((4,)), DMA((1,)),
            *both_ways(4, 4, 1, 1, 32, 2, NC, NC, NC),
        ],
        compiler_params=pltpu.CompilerParams(
            collective_id=0, has_side_effects=True, vmem_limit_bytes=60 * 1024 * 1024
        ),
        name="layer",
    )(*operands)


def local(
    queries,
    key_states,
    value_head_states,
    block_order,
    out_proj,
    residual,
    norm_gain,
    w_gate,
    w_up,
    w_down,
    routes,
    gate_weights,
):
    perm = jnp.asarray(slot_order(), BF)
    return layer(
        block_order, queries, key_states, value_head_states, out_proj, residual,
        norm_gain.reshape(1, D), routes.T, gate_weights.T, perm, w_gate, w_up, w_down,
    )


def solution(mesh):
    return jax.shard_map(
        local,
        mesh=mesh,
        in_specs=(
            P("ctx", "ep"),
            P("ctx", None),
            P("ctx", None),
            P("ctx"),
            P("ep", "ctx"),
            P(("ctx", "ep"), None),
            P(),
            P(None, ("ctx", "ep")),
            P(None, ("ctx", "ep")),
            P(("ctx", "ep"), None),
            P(("ctx", "ep"), None),
            P(("ctx", "ep"), None),
        ),
        out_specs=P(("ctx", "ep"), None),
        check_vma=False,
    )
```

time: 159 us -> 151 us (0.950)
  Pallas kernels: 156 us -> 149 us
    pallas_call x1, Pallas kernels: 156 us -> 149 us  [layer(): pl.pallas_call(layer_kernel, out_shape=SHAPE((ROWS, D), BF), in_specs=[SM...]
where the time goes in v3:
time: 151 us
  Pallas kernels  149 us (99%)
  local copies, waits for them, and re-layouts  1.57 us (1%)
    pallas_call x1, Pallas kernels, layer(): pl.pallas_call(layer_kernel, out_shape=SHAPE((ROWS, D), BF), in_specs=[SM...  149 us

profile of v3, /device:TPU:2, one launch (start us, length us, event | category | flops | bytes accessed | tf_op | source)
XLA Modules:
  0.0 151.0 jit_solution(9071787683432879920)
XLA Ops:
  0.0 149.4 %layer.1 = bf16[16,4096]{1,0:T(8,128)(2,1)} custom-call(s32[2]{0:T(128)} %order_ref.1, bf16[256,512]{1,0:T(8,128)(2,1)} %q_hbm.1, bf16[256,512]{1,0:T(8,128)(2,1)} %k_hbm.1, bf16[256,512]{1,0:T(8,128)(2,1)} %v_hbm.1, bf16[512,256]{1,0:T(8,128)(2,1)} %proj_hbm.1, bf16[16,4096]{1,0:T(8,128)(2,1)} %resid_hbm.1, f32[1,4096]{1,0:T(1,128)} %bitcast.3, ...), custom_call_target="tpu_custom_call" | custom-call | tf_op jit(solution)/shard_map/layer/pallas_call | solution.py:696
  149.4 1.6 %copy.15 = bf16[16,4096]{1,0:T(8,128)(2,1)} copy(bf16[16,4096]{1,0:T(8,128)(2,1)} %layer.1) | data formatting | bytes 262144

commit v4 on v3

--- a/solution.py
+++ b/solution.py
@@ -27,6 +27,7 @@
 SLOT = 8 * CAP
 SLOTS = 16 * SLOT
 FH = 384
+FAR_FIRST = sorted(range(1, 16), key=lambda i: -(min(i // 4, 4 - i // 4) + min(i % 4, 4 - i % 4)))
 
 
 def here():
@@ -59,27 +60,37 @@
     z = z_hi * 4 + z_lo
     partner = device(x, y, z_hi, z_lo, 1 - core)
 
+    def ahead(at, d, size):
+        return lax.rem(at + d, size) if d else at
+
+    ctx_at = [z_lo * 4 + ahead(y, d, 4) for d in range(4)]
+    ep_at = [z_hi * 8 + ahead(x, d, 4) * 2 + core for d in range(4)]
+    spans = [(ahead(z_lo, d, 4) * 4 + y, ep_at[0]) for d in range(4)]
+    across = (1 - z_hi) * 8 + x * 2 + core
+    columns_at = [
+        (lax.rem(ahead(z, d, 8), 4) * 4 + y, (ahead(z, d, 8) // 4) * 8 + x * 2 + core) for d in range(8)
+    ]
+
     def in_span(d):
-        return device(x, y, z_hi, (z_lo + d) % 4, core)
+        return spans[d]
 
     def along_y(d):
-        return device(x, (y + d) % 4, z_hi, z_lo, core)
+        return (ctx_at[d], ep_at[0])
 
     def along_x(d):
-        return device((x + d) % 4, y, z_hi, z_lo, core)
+        return (ctx_at[0], ep_at[d])
 
     def along_yz(dy, dz):
-        return device(x, (y + 4 - dy) % 4, (z_hi + dz) % 2, z_lo, core)
+        return (ctx_at[(4 - dy) % 4], across if dz else ep_at[0])
 
     def along_z(d):
-        to = (z + d) % 8
-        return device(x, y, to // 4, to % 4, core)
+        return columns_at[d % 8]
 
     def in_plane(i):
-        return device((x + i % 4) % 4, (y + i // 4) % 4, z_hi, z_lo, core)
+        return (ctx_at[i // 4], ep_at[i % 4])
 
     def plane_back(i):
-        return device((x + 4 - i % 4) % 4, (y + 4 - i // 4) % 4, z_hi, z_lo, core)
+        return (ctx_at[(4 - i // 4) % 4], ep_at[(4 - i % 4) % 4])
 
     def chunk(c):
         return pl.ds(pl.multiple_of(c * CW, CW), CW)
@@ -110,17 +121,11 @@
     def greet(target):
         pl.semaphore_signal(barrier, inc=1, device_id=target, device_id_type=MESH)
 
-    def greet_z(d, _):
+    greet(partner)
+    for d in range(1, 8):
         greet(along_z(d))
-        return 0
-
-    def greet_plane(i, _):
+    for i in range(1, 16):
         greet(in_plane(i))
-        return 0
-
-    greet(partner)
-    lax.fori_loop(1, 8, greet_z, 0)
-    lax.fori_loop(1, 16, greet_plane, 0)
     for dy in (1, 2, 3):
         greet(along_yz(dy, 1))
 
@@ -135,6 +140,33 @@
 
     loads[0].wait()
     loads[1].wait()
+    own_half = pl.ds(0, FH)
+    far_half = pl.ds(FH, FH)
+
+    def local_weights(f):
+        return (
+            pltpu.make_async_copy(wg_hbm.at[:, f], wg.at[f, :, :, own_half], lg.at[f]),
+            pltpu.make_async_copy(wu_hbm.at[:, f], wu.at[f, :, :, own_half], lu.at[f]),
+        )
+
+    def far_weights(f):
+        return (
+            remote(wg_hbm.at[:, f], wg.at[f, :, :, far_half], gs.at[f], gr.at[f], partner),
+            remote(wu_hbm.at[:, f], wu.at[f, :, :, far_half], us.at[f], ur.at[f], partner),
+        )
+
+    local_d = pltpu.make_async_copy(wd_hbm, wd.at[own_half, :], ld.at[0])
+    far_d = remote(wd_hbm, wd.at[far_half, :], ws.at[0], wr.at[0], partner)
+
+    def start_far(f):
+        for c in far_weights(f):
+            c.start()
+
+    for f in range(4):
+        for c in local_weights(f):
+            c.start()
+    local_d.start()
+
     pl.semaphore_wait(barrier, 26)
 
     def z_copy(d):
@@ -230,50 +262,7 @@
     def all_weigh():
         return remote(weigh.at[pl.ds(1, 7)], weigh_in.at[pl.ds(1, 7)], os_.at[0], or_.at[0], partner)
 
-    def send_weigh(d, _):
-        weigh_copy(d).start()
-        return 0
-
     weigh_in[0] = weigh[0]
-
-    own_half = pl.ds(0, FH)
-    far_half = pl.ds(FH, FH)
-
-    def from_rows(f, b):
-        return pl.ds(pl.multiple_of((b * 4 + f) * 256, 256), 256)
-
-    def local_weights(f):
-        for b in range(4):
-            pltpu.make_async_copy(wg_hbm.at[from_rows(f, b), :], wg.at[f, pl.ds(b * 256, 256), own_half], lg.at[f]).start()
-            pltpu.make_async_copy(wu_hbm.at[from_rows(f, b), :], wu.at[f, pl.ds(b * 256, 256), own_half], lu.at[f]).start()
-
-    def far_weights(f):
-        for b in range(4):
-            remote(wg_hbm.at[from_rows(f, b), :], wg.at[f, pl.ds(b * 256, 256), far_half], gs.at[f], gr.at[f], partner).start()
-            remote(wu_hbm.at[from_rows(f, b), :], wu.at[f, pl.ds(b * 256, 256), far_half], us.at[f], ur.at[f], partner).start()
-
-    def all_local(f):
-        return (
-            pltpu.make_async_copy(wg_hbm.at[pl.ds(0, 1024), :], wg.at[f, :, own_half], lg.at[f]),
-            pltpu.make_async_copy(wu_hbm.at[pl.ds(0, 1024), :], wu.at[f, :, own_half], lu.at[f]),
-        )
-
-    def all_far(f):
-        return (
-            remote(wg_hbm.at[pl.ds(0, 1024), :], wg.at[f, :, far_half], gs.at[f], gr.at[f], partner),
-            remote(wu_hbm.at[pl.ds(0, 1024), :], wu.at[f, :, far_half], us.at[f], ur.at[f], partner),
-        )
-
-    local_d = pltpu.make_async_copy(wd_hbm, wd.at[own_half, :], ld.at[0])
-    far_d = remote(wd_hbm, wd.at[far_half, :], ws.at[0], wr.at[0], partner)
-
-    def start_local(f, _):
-        local_weights(f)
-        return 0
-
-    def start_far(f, _):
-        far_weights(f)
-        return 0
 
     lanes = lax.broadcasted_iota(jnp.int32, (8, HEAD), 1).astype(F32)
     loads[3].wait()
@@ -338,16 +327,14 @@
         for dy in (1, 2, 3):
             y_copy(d, dy).wait_recv()
             core_copy(d, dy).start()
-        if d == 0:
-            lax.fori_loop(0, 4, start_local, 0)
-            local_d.start()
-        else:
+        if d > 0:
             if d == 1 or d == 3:
                 proj_arrival(d // 2)
                 proj_send(d // 2 + 1)
             group(d - 1, False)
     group(3, True)
-    lax.fori_loop(1, 8, send_weigh, 0)
+    for d in range(1, 8):
+        weigh_copy(d).start()
 
     def att_copy(dy):
         return remote(att.at[0], att.at[dy], as_.at[dy - 1], ar.at[dy - 1], along_y(dy))
@@ -399,13 +386,15 @@
     def token_copy(dy, slot, step):
         to = (slot + step) % 8
         return remote(
-            tok.at[dy, slot], tok.at[dy, to], ts.at[dy * 8 + to], tr.at[dy * 8 + to], along_z(1 if step == 1 else 7)
+            tok.at[dy, slot], tok.at[dy, to], ts.at[dy * 8 + to], tr.at[dy * 8 + to], along_z(step)
         )
 
     def last_step(dy):
-        return (3, 1) if dy % 2 == 0 else (5, 7)
+        return (3, 1) if dy == 1 else (5, 7)
 
     def token_moves(dy):
+        if dy in (0, 2):
+            return [[(0, d) for d in (4, 3, 5, 2, 6, 1, 7)]]
         return [[(0, 1), (0, 7)], [(1, 1), (7, 7)], [(2, 1), (6, 7)], [last_step(dy)]]
 
     def forward(dy, hop):
@@ -435,10 +424,12 @@
         return remote(packed.at[c], rows.at[c, pl.ds(1, 15)], xs.at[c], xr.at[c], partner)
 
     def pack(dy):
-        slot, step = last_step(dy)
-        token_copy(dy, slot, step).wait_recv()
-        slot, step = token_moves(dy)[2][1 if dy % 2 == 0 else 0]
-        token_copy(dy, slot, step).wait_recv()
+        if dy in (0, 2):
+            arriving = token_moves(dy)[0]
+        else:
+            arriving = [last_step(dy), token_moves(dy)[2][1 if dy == 1 else 0]]
+        for slot, step in arriving:
+            token_copy(dy, slot, step).wait_recv()
 
         def one(s, _):
             c = dy * SUB + s
@@ -453,11 +444,8 @@
 
             lax.fori_loop(0, CW // 256, columns, 0)
 
-            def send(i, _):
+            for i in FAR_FIRST:
                 remote(packed.at[c, i - 1], rows.at[c, i], xs.at[c], xr.at[c], in_plane(i)).start()
-                return 0
-
-            lax.fori_loop(1, 16, send, 0)
             return 0
 
         lax.fori_loop(0, SUB, one, 0)
@@ -485,34 +473,29 @@
 
     sum_cores(0)
     project(1)
-    sum_x(0)
     sum_cores(1)
     project(3)
+    start_far(0)
+    sum_x(0)
+    sum_cores(3)
+    project(2)
+    start_far(1)
     sum_x(1)
-    sum_cores(3)
+    sum_cores(2)
     square = sum_all(0, square)
-    project(2)
-    forward(0, 2)
+    start_far(2)
     sum_x(3)
-    sum_cores(2)
     square = sum_all(1, square)
-    forward(0, 3)
+    start_far(3)
     forward(1, 2)
-    forward(0, 4)
     sum_x(2)
+    pack(0)
     square = sum_all(3, square)
     forward(1, 3)
     forward(3, 2)
-    pack(0)
-    lax.fori_loop(0, 4, start_far, 0)
-    far_d.start()
     forward(1, 4)
     square = sum_all(2, square)
-    forward(3, 3)
-    forward(2, 2)
-    pack(1)
-    forward(3, 4)
-    forward(2, 3)
+    far_d.start()
     mean = jnp.sum(square, axis=1, keepdims=True) * (1.0 / D)
     factor = jnp.broadcast_to(lax.rsqrt(mean + EPS), (ROWS, 128))
     coarse = factor.astype(BF)
@@ -521,8 +504,10 @@
     scale[0] = jnp.where(lane < 64, coarse.astype(F32), fine.astype(F32)).astype(BF)
     for d in range(1, 8):
         scale_copy(d).start()
+    forward(3, 3)
+    pack(1)
+    forward(3, 4)
     pack(3)
-    forward(2, 4)
     pack(2)
 
     all_scales().wait_recv()
@@ -531,23 +516,17 @@
     scale_in[0] = got[0]
     scale_out[...] = got[1:]
 
-    def send_scale(i, _):
+    for i in range(1, 16):
         remote(scale_out.at[i - 1], scale_in.at[i], ss.at[1], sr.at[1], in_plane(i)).start()
-        return 0
-
-    lax.fori_loop(1, 16, send_scale, 0)
 
     acc_g[...] = jnp.zeros_like(acc_g)
     acc_u[...] = jnp.zeros_like(acc_u)
 
-    def weights_here(f, _):
-        for c in all_local(f):
+    for f in range(4):
+        for c in local_weights(f):
             c.wait()
-        for c in all_far(f):
+        for c in far_weights(f):
             c.wait_recv()
-        return 0
-
-    lax.fori_loop(0, 4, weights_here, 0)
 
     def upward(s, dy):
         c = dy * SUB + s
@@ -557,11 +536,11 @@
             f = (y + 4 - q + dy) % 4
             got = rows[c, pl.ds(q * 4, 4)].reshape(4 * SLOT, CW)
             at = pl.ds(pl.multiple_of(q * 4 * SLOT, 4 * SLOT), 4 * SLOT)
-            depth = pl.ds(pl.multiple_of(s * CW, CW), CW)
+            depth = pl.ds(s * 2, 2)
             for n in range(3):
                 cols = slice(n * 256, n * 256 + 256)
-                acc_g[at, cols] += jnp.dot(got, wg[f, depth, cols], preferred_element_type=F32)
-                acc_u[at, cols] += jnp.dot(got, wu[f, depth, cols], preferred_element_type=F32)
+                acc_g[at, cols] += jnp.dot(got, wg[f, depth, :, cols].reshape(CW, 256), preferred_element_type=F32)
+                acc_u[at, cols] += jnp.dot(got, wu[f, depth, :, cols].reshape(CW, 256), preferred_element_type=F32)
             return 0
 
         lax.fori_loop(0, 4, one, 0)
@@ -597,44 +576,11 @@
 
         lax.fori_loop(0, CW // 256, columns, 0)
 
-        def send(i, _):
+        for i in FAR_FIRST:
             remote(back.at[c, i - 1], ret.at[c, i], rs.at[c], rr.at[c], plane_back(i)).start()
-            return 0
-
-        lax.fori_loop(1, 16, send, 0)
         return 0
 
     lax.fori_loop(0, NC, downward, 0)
-
-    def combine(c, _):
-        all_back(c).wait_recv()
-
-        def columns(n, _):
-            got = ret[c, :, :, tile(n)].reshape(SLOTS, 256)
-            got = jnp.dot(spread[...], got, preferred_element_type=F32)
-            summed[c, :, :, tile(n)] = got.astype(BF).reshape(8, ROWS, 256)
-            return 0
-
-        lax.fori_loop(0, CW // 256, columns, 0)
-
-        def send(d, _):
-            remote(summed.at[c, d], sums_in.at[c, d], fs.at[c], fr.at[c], along_z(8 - d)).start()
-            return 0
-
-        lax.fori_loop(1, 8, send, 0)
-        return 0
-
-    lax.fori_loop(0, NC, combine, 0)
-
-    def finish(c, _):
-        all_sums(c).wait_recv()
-        got = summed[c, 0].astype(F32)
-        for d in range(1, 8):
-            got = got + sums_in[c, d].astype(F32)
-        out_ref[:, chunk(c)] = (hidden[:, chunk(c)].astype(F32) + got).astype(BF)
-        return 0
-
-    lax.fori_loop(0, NC, finish, 0)
 
     for d in (1, 2, 3):
         z_copy(d).wait_send()
@@ -656,20 +602,52 @@
         for moves in token_moves(dy):
             for slot, step in moves:
                 token_copy(dy, slot, step).wait_send()
-        for c in all_far(dy):
+        for c in far_weights(dy):
             c.wait_send()
     all_weigh().wait_send()
     all_scales().wait_send()
     all_slot_scales().wait_send()
 
+    def drain_rows(c, _):
+        all_rows(c).wait_send()
+        return 0
+
+    lax.fori_loop(0, NC, drain_rows, 0)
+    far_d.wait_send()
+
+    def combine(c, _):
+        all_back(c).wait_recv()
+
+        def columns(n, _):
+            got = ret[c, :, :, tile(n)].reshape(SLOTS, 256)
+            got = jnp.dot(spread[...], got, preferred_element_type=F32)
+            summed[c, :, :, tile(n)] = got.astype(BF).reshape(8, ROWS, 256)
+            return 0
+
+        lax.fori_loop(0, CW // 256, columns, 0)
+
+        for d in (4, 3, 5, 2, 6, 1, 7):
+            remote(summed.at[c, d], sums_in.at[c, d], fs.at[c], fr.at[c], along_z(8 - d)).start()
+        return 0
+
+    lax.fori_loop(0, NC, combine, 0)
+
+    def finish(c, _):
+        all_sums(c).wait_recv()
+        got = summed[c, 0].astype(F32)
+        for d in range(1, 8):
+            got = got + sums_in[c, d].astype(F32)
+        out_ref[:, chunk(c)] = (hidden[:, chunk(c)].astype(F32) + got).astype(BF)
+        return 0
+
+    lax.fori_loop(0, NC, finish, 0)
+
     def drain(c, _):
-        all_rows(c).wait_send()
         all_back(c).wait_send()
         all_sums(c).wait_send()
         return 0
 
     lax.fori_loop(0, NC, drain, 0)
-    far_d.wait_send()
 
 
 def slot_order():
@@ -720,8 +698,8 @@
             pltpu.VMEM((4, 2, ROWS, 1024), BF),
             pltpu.VMEM((4, 2, ROWS, 1024), BF),
             pltpu.VMEM((ROWS, D), BF),
-            pltpu.VMEM((4, 1024, 2 * FH), BF),
-            pltpu.VMEM((4, 1024, 2 * FH), BF),
+            pltpu.VMEM((4, 4, 256, 2 * FH), BF),
+            pltpu.VMEM((4, 4, 256, 2 * FH), BF),
             pltpu.VMEM((2 * FH, D), BF),
             pltpu.VMEM((8, CAP, 16, 128), BF),
             pltpu.VMEM((8, CAP, 16, 128), BF),
@@ -769,7 +747,8 @@
     perm = jnp.asarray(slot_order(), BF)
     return layer(
         block_order, queries, key_states, value_head_states, out_proj, residual,
-        norm_gain.reshape(1, D), routes.T, gate_weights.T, perm, w_gate, w_up, w_down,
+        norm_gain.reshape(1, D), routes.T, gate_weights.T, perm,
+        w_gate.reshape(4, 4, 256, FH), w_up.reshape(4, 4, 256, FH), w_down,
     )
 
 

time: 151 us -> 149 us (0.987)
  Pallas kernels: 149 us -> 147 us
    pallas_call x1, Pallas kernels: 149 us -> 147 us  [layer(): pl.pallas_call(layer_kernel, out_shape=SHAPE((ROWS, D), BF), in_specs=[SM...]
where the time goes in v4:
time: 149 us
  Pallas kernels  147 us (99%)
  local copies, waits for them, and re-layouts  1.57 us (1%)
    pallas_call x1, Pallas kernels, layer(): pl.pallas_call(layer_kernel, out_shape=SHAPE((ROWS, D), BF), in_specs=[SM...  147 us

profile of v4, /device:TPU:2, one launch (start us, length us, event | category | flops | bytes accessed | tf_op | source)
XLA Modules:
  0.0 148.9 jit_solution(13857906656086129637)
XLA Ops:
  0.0 147.3 %layer.1 = bf16[16,4096]{1,0:T(8,128)(2,1)} custom-call(s32[2]{0:T(128)} %order_ref.1, bf16[256,512]{1,0:T(8,128)(2,1)} %q_hbm.1, bf16[256,512]{1,0:T(8,128)(2,1)} %k_hbm.1, bf16[256,512]{1,0:T(8,128)(2,1)} %v_hbm.1, bf16[512,256]{1,0:T(8,128)(2,1)} %proj_hbm.1, bf16[16,4096]{1,0:T(8,128)(2,1)} %resid_hbm.1, f32[1,4096]{1,0:T(1,128)} %bitcast.7, ...), custom_call_target="tpu_custom_call" | custom-call | tf_op jit(solution)/shard_map/layer/pallas_call | solution.py:674
  147.3 1.6 %copy.15 = bf16[16,4096]{1,0:T(8,128)(2,1)} copy(bf16[16,4096]{1,0:T(8,128)(2,1)} %layer.1) | data formatting | bytes 262144

commit v5 on v4

--- a/solution.py
+++ b/solution.py
@@ -250,7 +250,7 @@
 
     for d in (1, 2, 3):
         z_copy(d).wait_recv()
-        if d == 1:
+        if d == 3:
             loads[2].wait()
             proj_send(0)
         for dy in (1, 2, 3):

time: 149 us -> 151 us (1.013)
  Pallas kernels: 147 us -> 149 us
where the time goes in v5:
time: 151 us; the launch traced here: 150 us
  Pallas kernels  149 us (99%)
  local copies, waits for them, and re-layouts  1.57 us (1%)
    pallas_call x1, Pallas kernels, layer(): pl.pallas_call(layer_kernel, out_shape=SHAPE((ROWS, D), BF), in_specs=[SM...  149 us

profile of v5, /device:TPU:2, one launch (start us, length us, event | category | flops | bytes accessed | tf_op | source)
XLA Modules:
  0.0 150.2 jit_solution(4698696053280523335)
XLA Ops:
  0.0 148.6 %layer.1 = bf16[16,4096]{1,0:T(8,128)(2,1)} custom-call(s32[2]{0:T(128)} %order_ref.1, bf16[256,512]{1,0:T(8,128)(2,1)} %q_hbm.1, bf16[256,512]{1,0:T(8,128)(2,1)} %k_hbm.1, bf16[256,512]{1,0:T(8,128)(2,1)} %v_hbm.1, bf16[512,256]{1,0:T(8,128)(2,1)} %proj_hbm.1, bf16[16,4096]{1,0:T(8,128)(2,1)} %resid_hbm.1, f32[1,4096]{1,0:T(1,128)} %bitcast.7, ...), custom_call_target="tpu_custom_call" | custom-call | tf_op jit(solution)/shard_map/layer/pallas_call | solution.py:674
  148.6 1.6 %copy.15 = bf16[16,4096]{1,0:T(8,128)(2,1)} copy(bf16[16,4096]{1,0:T(8,128)(2,1)} %layer.1) | data formatting | bytes 262144
